TPU v7x, 1024 devices: a whole 4x8x16 slice. The times are simulated.
1024 devices in a mesh: expert: 64 (over z, x), tensor: 16 (over y, core).
Axes of the slice: x: 4, y: 8, z: 16, core: 2. Of those that a mesh axis runs over, the one named last changes fastest.
Arguments:
- tokens: bfloat16 [4096, 1536], P('expert'), may hold values from -6 to 6
- exponents: int32 [4096, 12], P('expert'), may hold values from -1 to 1
- out_grad: bfloat16 [4096, 1536], P('expert'), may hold values from -6 to 6
- slots: int32 [64, 128], replicated, may hold values from 0 to 4095, as said below
- gates: float32 [64, 128], P('expert'), may hold values from 0.1 to 1
- w_in: bfloat16 [64, 1536, 4096], P('expert', None, 'tensor'), may hold values from -0.15625 to 0.15625
- w_out: bfloat16 [64, 4096, 1536], P('expert', 'tensor'), may hold values from -0.09375 to 0.09375
Outputs:
- token_grad: bfloat16 [4096, 1536], P(('expert', 'tensor'))
- w_in_grad: bfloat16 [64, 1536, 4096], P('expert', None, 'tensor')
- w_out_grad: bfloat16 [64, 4096, 1536], P('expert', 'tensor')
- gate_grad: float32 [64, 128], P('expert')
Inputs may be any that keep to these rules, and one draw needn't show every extreme that they name: `slots`: each row holds 128 distinct token indices. In every row, at most 2 indices fall in any aligned block of 64 tokens (the tokens of one index of expert), and some block holds exactly 2.
All inputs are finite; a program needn't handle non-finite values.
Results may differ from a plain program's by a relative error of at most 0.007.
Values may be sent and summed in bfloat16 or wider, within the bound.
No kernel may reach another device: no remote copies, remote signals or barrier semaphores. Data moves between devices by JAX's collectives and lax.ppermute only.
A program may use at most 32 MiB of HBM per device.

v0:
```python
import jax
import jax.numpy as jnp
from jax import lax
from jax.sharding import PartitionSpec as P


def contract(left, right, left_dim, right_dim):
    return lax.dot_general(
        left, right, (((left_dim,), (right_dim,)), ((), ())), preferred_element_type=jnp.float32
    )


def apply_scales(values, exponents):
    row_count = values.shape[0]
    block_count = exponents.shape[1]
    factors = jnp.exp2(exponents.astype(jnp.float32))
    widened = values.astype(jnp.float32).reshape(row_count, block_count, 128) * factors[:, :, None]
    return widened.reshape(row_count, block_count * 128)


def local(tokens, exponents, out_grad, slots, gates, w_in, w_out):
    expert_count = lax.axis_size("expert")
    my_expert = lax.axis_index("expert")
    my_tensor = lax.axis_index("tensor")
    tok_count = tokens.shape[0]
    model_width = tokens.shape[1]
    slot_count = slots.shape[1]
    capacity = slot_count // expert_count + slot_count // (4 * expert_count)
    total_slots = expert_count * capacity
    owner = slots // tok_count
    local_index = slots % tok_count
    from_here = owner == my_expert
    send_order = jnp.cumsum(from_here.astype(jnp.int32), axis=1) - 1
    rank_range = jnp.arange(capacity, dtype=jnp.int32)
    send_hit = from_here[:, :, None] & (send_order[:, :, None] == rank_range[None, None, :])
    send_valid = jnp.any(send_hit, axis=1)
    picked_index = jnp.sum(jnp.where(send_hit, local_index[:, :, None], 0), axis=1)
    send_table = jnp.where(send_valid, picked_index, tok_count)
    row_owner = lax.dynamic_index_in_dim(owner, my_expert, 0, keepdims=False)
    slot_range = jnp.arange(slot_count, dtype=jnp.int32)
    earlier = (row_owner[:, None] == row_owner[None, :]) & (
        slot_range[:, None] > slot_range[None, :]
    )
    row_rank = jnp.sum(earlier.astype(jnp.int32), axis=1)
    flat_index = row_owner * capacity + row_rank
    scaled_local = apply_scales(tokens, exponents).astype(jnp.bfloat16)
    sent_rows = jnp.take(scaled_local, send_table, axis=0, mode="fill", fill_value=0)
    sent_grads = jnp.take(out_grad, send_table, axis=0, mode="fill", fill_value=0)
    arrived_rows, arrived_grads = (
        lax.all_to_all(sent_rows, "expert", split_axis=0, concat_axis=0, tiled=True),
        lax.all_to_all(sent_grads, "expert", split_axis=0, concat_axis=0, tiled=True),
    )
    slot_rows = arrived_rows.reshape(total_slots, model_width)
    slot_grads = arrived_grads.reshape(total_slots, model_width)
    gate_row = jnp.zeros((total_slots,), jnp.float32).at[flat_index].set(gates[0])
    weight_in = w_in[0]
    weight_out = w_out[0]
    preact = jnp.dot(slot_rows, weight_in, preferred_element_type=jnp.float32)
    hidden_full, backward = jax.vjp(jax.nn.gelu, preact)
    hidden = hidden_full.astype(jnp.bfloat16)
    upstream = contract(slot_grads, weight_out, 1, 1)
    gate_part = jnp.sum(hidden.astype(jnp.float32) * upstream, axis=1)
    gate_total = lax.psum(gate_part[flat_index], "tensor")
    dpre = backward(gate_row[:, None] * upstream)[0].astype(jnp.bfloat16)
    gated_grads = (gate_row[:, None] * slot_grads.astype(jnp.float32)).astype(jnp.bfloat16)
    out_weight_grad = contract(hidden, gated_grads, 0, 0).astype(jnp.bfloat16)
    in_weight_grad = contract(slot_rows, dpre, 0, 0).astype(jnp.bfloat16)
    slot_back = contract(dpre, weight_in, 1, 1)
    flat_send = send_table.reshape(-1)
    came_back = lax.all_to_all(
        slot_back.reshape(expert_count, capacity, model_width),
        "expert",
        split_axis=0,
        concat_axis=0,
        tiled=True,
    )
    token_sums = (
        jnp.zeros((tok_count, model_width), jnp.float32)
        .at[flat_send]
        .add(came_back.reshape(total_slots, model_width), mode="drop")
    )
    my_share = lax.psum_scatter(token_sums, "tensor", scatter_dimension=0, tiled=True)
    share_rows = my_share.shape[0]
    my_scales = lax.dynamic_slice_in_dim(exponents, my_tensor * share_rows, share_rows, 0)
    token_grad = apply_scales(my_share, my_scales).astype(jnp.bfloat16)
    return (token_grad, in_weight_grad[None], out_weight_grad[None], gate_total[None])


def solution(mesh):
    placed = (
        P("expert", None),
        P("expert", None),
        P("expert", None),
        P(),
        P("expert", None),
        P("expert", None, "tensor"),
        P("expert", "tensor", None),
    )
    return jax.shard_map(
        local,
        mesh=mesh,
        in_specs=placed,
        out_specs=(
            P(("expert", "tensor"), None),
            P("expert", None, "tensor"),
            P("expert", "tensor", None),
            P("expert", None),
        ),
        check_vma=False,
    )
```

profile of v0, /device:TPU:1, one launch (start us, length us, event | category | flops | bytes accessed | tf_op | source)
XLA Modules:
  0.0 277.0 jit_solution(17138705400196827782)
XLA Ops:
  7.2 0.9 fusion.31
  8.1 0.3 reduce_window_sum.11
  8.4 0.8 add_select_fusion
  9.7 0.9 gather_fusion.1
  10.6 0.1 reshape.153
  10.9 0.4 copy-done.3
  11.4 0.2 mul.109
  11.7 0.9 gather_fusion.2
  12.6 0.2 reshape.157
  12.8 1.5 broadcast_select_fusion.1
  14.3 47.5 %all_to_all.15 = bf16[64,2,1536]{2,1,0:T(2,128)(2,1)S(1)} all-to-all(bf16[64,2,1536]{2,1,0:T(2,128)(2,1)S(1)} %get-tuple-element.13), channel_id=1, replica_groups=mesh['expert'=64,'tensor'=16] {'expert'}, dimensions={0} | all-to-all | bytes 786432 | tf_op jit(solution)/shard_map/all_to_all | solution.py:50
  61.8 7.5 %all-to-all-start = ((bf16[64,2,1536]{2,1,0:T(2,128)(2,1)}), bf16[64,2,1536]{2,1,0:T(2,128)(2,1)S(1)}, u32[]{:S(2)}, u32[]{:S(2)}) async-start(bf16[64,2,1536]{2,1,0:T(2,128)(2,1)} %get-tuple-element.12), calls=%async_computation | async-start | bytes 786432 | tf_op jit(solution)/shard_map/all_to_all | solution.py:51
  69.3 0.2 convert_reduce_fusion
  69.5 1.1 scatter_custom_fusion
  70.6 0.1 reshape.104
  70.8 0.3 fusion.4
  71.1 21.9 %all-to-all-done = bf16[64,2,1536]{2,1,0:T(2,128)(2,1)S(1)} async-done(((bf16[64,2,1536]{2,1,0:T(2,128)(2,1)}), bf16[64,2,1536]{2,1,0:T(2,128)(2,1)S(1)}, u32[]{:S(2)}, u32[]{:S(2)}) %all-to-all-start) | async-done | bytes 393248 | tf_op jit(solution)/shard_map/all_to_all | solution.py:51
  92.9 0.1 reshape.103
  93.1 0.5 multiply_reduce_fusion
  93.7 0.4 fusion.2
  94.0 1.5 copy.38
  95.5 8.8 %all-to-all-start.2 = ((f32[64,2,1536]{2,1,0:T(2,128)}), f32[64,2,1536]{2,1,0:T(2,128)S(1)}, u32[]{:S(2)}, u32[]{:S(2)}) async-start(f32[64,2,1536]{2,1,0:T(2,128)} %copy.38), calls=%async_computation.2 | async-start | bytes 1572864 | tf_op jit(solution)/shard_map/all_to_all | solution.py:70
  104.8 1.3 dynamic-slice
  106.8 37.4 %all-to-all-done.2 = f32[64,2,1536]{2,1,0:T(2,128)S(1)} async-done(((f32[64,2,1536]{2,1,0:T(2,128)}), f32[64,2,1536]{2,1,0:T(2,128)S(1)}, u32[]{:S(2)}, u32[]{:S(2)}) %all-to-all-start.2) | async-done | bytes 786464 | tf_op jit(solution)/shard_map/all_to_all | solution.py:70
  144.2 0.5 reshape.142
  144.8 2.5 scatter_custom_fusion.1
  147.3 1.3 fusion
  148.6 1.2 gather_fusion
  149.8 29.1 %psum.7 = f32[1,128]{1,0:T(1,128)} all-reduce(f32[1,128]{1,0:T(1,128)S(1)} %bitcast.46), channel_id=1, replica_groups=mesh['expert'=64,'tensor'=16] {'tensor'}, use_global_device_ids=true, to_apply=%region_8.10 | all-reduce | flops 128 | bytes 1024 | tf_op jit(solution)/shard_map/psum | solution.py:63
  179.0 1.3 fusion.1
  180.3 88.5 %all-reduce.3.cloned.1.call-done = f32[64,1536]{1,0:T(8,128)} async-done(((f32[64,1536]{1,0:T(8,128)}), f32[64,1536]{1,0:T(8,128)}) %all-reduce.3.cloned.1.call-update) | async-done | bytes 393232
  268.8 1.4 fusion.24
  (33 shorter events, 1.5 us)
Async XLA Ops:
  7.2 63.6 %copy-start = (bf16[1,1536,256]{2,1,0:T(8,128)(2,1)S(1)}, bf16[1,1536,256]{2,1,0:T(8,128)(2,1)}, u32[]{:S(2)}) copy-start(bf16[1,1536,256]{2,1,0:T(8,128)(2,1)} %param.14) | copy-start | bytes 2359300
  7.2 2.5 copy-start.1
  10.6 0.7 copy-start.3
  10.6 1.0 copy-start.2
  61.8 31.1 %all-to-all-start = ((bf16[64,2,1536]{2,1,0:T(2,128)(2,1)}), bf16[64,2,1536]{2,1,0:T(2,128)(2,1)S(1)}, u32[]{:S(2)}, u32[]{:S(2)}) async-start(bf16[64,2,1536]{2,1,0:T(2,128)(2,1)} %get-tuple-element.12), calls=%async_computation | async-start | bytes 786432 | tf_op jit(solution)/shard_map/all_to_all | solution.py:51
  70.8 22.3 %copy-start.4 = (bf16[1,256,1536]{2,1,0:T(8,128)(2,1)S(1)}, bf16[1,256,1536]{2,1,0:T(8,128)(2,1)}, u32[]{:S(2)}) copy-start(bf16[1,256,1536]{2,1,0:T(8,128)(2,1)} %param.15) | copy-start | bytes 2359300
  95.5 48.7 %all-to-all-start.2 = ((f32[64,2,1536]{2,1,0:T(2,128)}), f32[64,2,1536]{2,1,0:T(2,128)S(1)}, u32[]{:S(2)}, u32[]{:S(2)}) async-start(f32[64,2,1536]{2,1,0:T(2,128)} %copy.38), calls=%async_computation.2 | async-start | bytes 1572864 | tf_op jit(solution)/shard_map/all_to_all | solution.py:70
  104.3 164.4 %all-reduce.3.cloned.1.call-start = ((), (), s32[]{:S(2)}) async-start(), calls=%async_computation.3 | async-start | bytes 786432
Sparse Core Ops, SparseCore 0:
  147.5 121.2 all-reduce.2
where the time goes:
time: 278 us; the launch traced here: 277 us
  waiting for transfers between devices  148 us (53%)
  blocking collectives  76.6 us (28%)
  starting transfers between devices  16.3 us (6%)
  between operations  14.9 us (5%)
  local copies, waits for them, and re-layouts  9.61 us (3%)
  other arithmetic  8.03 us (3%)
  matrix products  3.75 us (1%)
    unnamed x2, waiting for transfers between devices  88.5 us
    all_to_all x1, blocking collectives, local(): lax.all_to_all(sent_rows, 'expert', split_axis=0, concat_axis=0, tiled=True)  47.5 us
    all_to_all x1, waiting for transfers between devices, local(): lax.all_to_all(slot_back.reshape(expert_count, capacity, model_width), 'e...  37.4 us
    psum x1, blocking collectives, local(): gate_total = lax.psum(gate_part[flat_index], 'tensor')  29.1 us
    all_to_all x1, waiting for transfers between devices, local(): lax.all_to_all(sent_grads, 'expert', split_axis=0, concat_axis=0, tiled=T...  21.9 us
    all_to_all x1, starting transfers between devices, local(): lax.all_to_all(slot_back.reshape(expert_count, capacity, model_width), 'e...  8.77 us
    all_to_all x1, starting transfers between devices, local(): lax.all_to_all(sent_grads, 'expert', split_axis=0, concat_axis=0, tiled=T...  7.46 us
  transfers between devices with their start and end apart: 3, of which 3 were waited for; matrix products, arithmetic and copies ran while one was open for 3% of the time, Pallas kernels for 0%

commit v1 on v0

v1 whole, which is shorter than its diff:
```python
import jax
import jax.numpy as jnp
from jax import lax
from jax.sharding import PartitionSpec as P


def contract(left, right, left_dim, right_dim):
    return lax.dot_general(
        left, right, (((left_dim,), (right_dim,)), ((), ())), preferred_element_type=jnp.float32
    )


def apply_scales(values, exponents):
    row_count = values.shape[0]
    block_count = exponents.shape[1]
    factors = jnp.exp2(exponents.astype(jnp.float32))
    widened = values.astype(jnp.float32).reshape(row_count, block_count, 128) * factors[:, :, None]
    return widened.reshape(row_count, block_count * 128)


def local(tokens, exponents, out_grad, slots, gates, w_in, w_out):
    expert_count = lax.axis_size("expert")
    tensor_count = lax.axis_size("tensor")
    my_expert = lax.axis_index("expert")
    my_tensor = lax.axis_index("tensor")
    core = my_tensor % 2
    swap = [(index, index ^ 1) for index in range(tensor_count)]
    tok_count, width = tokens.shape
    half = width // 2
    half_blocks = exponents.shape[1] // 2
    slot_count = slots.shape[1]

    local_index = slots % tok_count
    from_here = slots // tok_count == my_expert
    lower = jnp.min(jnp.where(from_here, local_index, tok_count), axis=1)
    upper = jnp.max(jnp.where(from_here, local_index, -1), axis=1)
    picked = jnp.stack([lower, upper], axis=1).reshape(slot_count)
    pick = (picked[:, None] == jnp.arange(tok_count)[None, :]).astype(jnp.bfloat16)

    scaled = apply_scales(
        lax.dynamic_slice_in_dim(tokens, core * half, half, 1),
        lax.dynamic_slice_in_dim(exponents, core * half_blocks, half_blocks, 1),
    ).astype(jnp.bfloat16)
    both = jnp.concatenate([scaled, lax.dynamic_slice_in_dim(out_grad, core * half, half, 1)], axis=1)
    sent = contract(pick, both, 1, 0).astype(jnp.bfloat16).reshape(expert_count, 2, width)
    mine = lax.all_to_all(sent, "expert", split_axis=0, concat_axis=0, tiled=True)
    mine = mine.reshape(slot_count, width)
    other = lax.ppermute(mine, "tensor", swap)
    first = jnp.where(core == 0, mine, other)
    second = jnp.where(core == 0, other, mine)
    slot_rows = jnp.concatenate([first[:, :half], second[:, :half]], axis=1)
    slot_grads = jnp.concatenate([first[:, half:], second[:, half:]], axis=1)

    my_slots = lax.dynamic_index_in_dim(slots, my_expert, 0, keepdims=False)
    rank = jnp.sum((my_slots[:, None] > my_slots[None, :]).astype(jnp.int32), axis=1)
    placed = rank[None, :] == jnp.arange(slot_count)[:, None]
    gate_row = jnp.sum(jnp.where(placed, gates, 0.0), axis=1)
    weight_in = w_in[0]
    weight_out = w_out[0]
    preact = jnp.dot(slot_rows, weight_in, preferred_element_type=jnp.float32)
    hidden_full, backward = jax.vjp(jax.nn.gelu, preact)
    hidden = hidden_full.astype(jnp.bfloat16)
    upstream = contract(slot_grads, weight_out, 1, 1)
    gate_part = jnp.sum(hidden.astype(jnp.float32) * upstream, axis=1)
    gate_part = jnp.sum(jnp.where(placed, gate_part[:, None], 0.0), axis=0)
    dpre = backward(gate_row[:, None] * upstream)[0].astype(jnp.bfloat16)
    gated_grads = (gate_row[:, None] * slot_grads.astype(jnp.float32)).astype(jnp.bfloat16)

    keep_weight = lax.dynamic_slice_in_dim(weight_in, core * half, half, 0)
    give_weight = lax.dynamic_slice_in_dim(weight_in, (1 - core) * half, half, 0)
    given = contract(dpre, give_weight, 1, 1).astype(jnp.bfloat16)
    taken = lax.ppermute(given, "tensor", swap)
    chip_back = (contract(dpre, keep_weight, 1, 1) + taken.astype(jnp.float32)).astype(jnp.bfloat16)
    came_back = lax.all_to_all(
        chip_back.reshape(expert_count, 2, half), "expert", split_axis=0, concat_axis=0, tiled=True
    )
    out_weight_grad = contract(hidden, gated_grads, 0, 0).astype(jnp.bfloat16)
    in_weight_grad = contract(slot_rows, dpre, 0, 0).astype(jnp.bfloat16)
    token_sums = contract(pick, came_back.reshape(slot_count, half), 0, 0).astype(jnp.bfloat16)

    share = tok_count // tensor_count
    gate_high = gate_part.astype(jnp.bfloat16)
    gate_low = (gate_part - gate_high.astype(jnp.float32)).astype(jnp.bfloat16)
    gate_rows = jnp.zeros((share, slot_count), jnp.bfloat16).at[0].set(gate_high).at[1].set(gate_low)
    packed = jnp.concatenate(
        [
            token_sums.reshape(tensor_count, share, half),
            jnp.broadcast_to(gate_rows[None], (tensor_count, share, slot_count)),
        ],
        axis=2,
    )
    arrived = lax.all_to_all(packed, "tensor", split_axis=0, concat_axis=0, tiled=True)
    summed = jnp.sum(arrived.astype(jnp.float32).reshape(tensor_count // 2, 2, share, -1), axis=0)
    my_share = jnp.concatenate([summed[0, :, :half], summed[1, :, :half]], axis=1)
    gate_total = jnp.sum(summed[:, :2, half:], axis=(0, 1))
    my_scales = lax.dynamic_slice_in_dim(exponents, my_tensor * share, share, 0)
    token_grad = apply_scales(my_share, my_scales).astype(jnp.bfloat16)
    return (token_grad, in_weight_grad[None], out_weight_grad[None], gate_total[None])


def solution(mesh):
    placed = (
        P("expert", None),
        P("expert", None),
        P("expert", None),
        P(),
        P("expert", None),
        P("expert", None, "tensor"),
        P("expert", "tensor", None),
    )
    return jax.shard_map(
        local,
        mesh=mesh,
        in_specs=placed,
        out_specs=(
            P(("expert", "tensor"), None),
            P("expert", None, "tensor"),
            P("expert", "tensor", None),
            P("expert", None),
        ),
        check_vma=False,
    )
```

time: 278 us -> 112 us (0.40)
  waiting for transfers between devices: 148 us -> 25 us
  blocking collectives: 76.6 us -> 47.5 us
  between operations: 14.9 us -> 0.86 us
  starting transfers between devices: 16.3 us -> 23.4 us
  local copies, waits for them, and re-layouts: 9.61 us -> 5.18 us
  other arithmetic: 8.03 us -> 4.5 us
    unnamed x2 -> x0, waiting for transfers between devices: 88.5 us -> none
    all_to_all x2, waiting for transfers between devices: 59.3 us -> 23.6 us  [the longest x1 17.3 us: local(): lax.all_to_all(chip_back.reshape(expert_count, 2, half), 'expert', split_...]
    psum x1 -> x0, blocking collectives: 29.1 us -> none  [local(): gate_total = lax.psum(gate_part[flat_index], 'tensor')]
    ppermute x0 -> x2, starting transfers between devices: none -> 7.55 us  [the longest x1 5.27 us: local(): other = lax.ppermute(mine, 'tensor', swap)]
    gather x5 -> x0, local copies, waits for them, and re-layouts: 3.32 us -> none  [the longest x1 1.22 us: local(): gate_total = lax.psum(gate_part[flat_index], 'tensor')]
  transfers between devices with their start and end apart: 3 -> 4, of which waited for: 3 -> 4; matrix products, arithmetic and copies ran while one was open for 3% -> 3% of each run, Pallas kernels for 0% -> 0%
where the time goes in v1:
time: 112 us; the launch traced here: 111 us
  blocking collectives  47.5 us (42%)
  waiting for transfers between devices  25 us (22%)
  starting transfers between devices  23.4 us (21%)
  local copies, waits for them, and re-layouts  5.18 us (5%)
  other arithmetic  4.5 us (4%)
  matrix products  4.5 us (4%)
    all_to_all x1, blocking collectives, local(): lax.all_to_all(sent, 'expert', split_axis=0, concat_axis=0, tiled=True)  47.5 us
    all_to_all x1, waiting for transfers between devices, local(): lax.all_to_all(chip_back.reshape(expert_count, 2, half), 'expert', split_...  17.3 us
    all_to_all x1, starting transfers between devices, local(): lax.all_to_all(packed, 'tensor', split_axis=0, concat_axis=0, tiled=True)  10.4 us
    all_to_all x1, waiting for transfers between devices, local(): lax.all_to_all(packed, 'tensor', split_axis=0, concat_axis=0, tiled=True)  6.23 us
    all_to_all x1, starting transfers between devices, local(): lax.all_to_all(chip_back.reshape(expert_count, 2, half), 'expert', split_...  5.44 us
    ppermute x1, starting transfers between devices, local(): other = lax.ppermute(mine, 'tensor', swap)  5.27 us
    dot_general x7, matrix products, contract(): lax.dot_general(left, right, (((left_dim,), (right_dim,)), ((), ())), pre...  4.23 us
    ppermute x1, starting transfers between devices, local(): taken = lax.ppermute(given, 'tensor', swap)  2.29 us
  transfers between devices with their start and end apart: 4, of which 4 were waited for; matrix products, arithmetic and copies ran while one was open for 3% of the time, Pallas kernels for 0%

profile of v1, /device:TPU:1, one launch (start us, length us, event | category | flops | bytes accessed | tf_op | source)
XLA Modules:
  0.0 111.0 jit_solution(4718613684291814506)
XLA Ops:
  0.7 0.8 multiply_exponential_fusion
  1.5 0.9 select_reduce_fusion.3
  2.6 0.1 eq.44
  2.7 0.9 constant_dynamic-slice_fusion.1
  3.7 0.9 fusion.14
  4.7 0.3 convolution_convert_fusion.2
  5.0 0.1 reshape.120
  5.2 47.5 %all_to_all.15 = bf16[64,2,1536]{2,1,0:T(2,128)(2,1)S(1)} all-to-all(bf16[64,2,1536]{2,1,0:T(2,128)(2,1)S(1)} %reshape.120), channel_id=1, replica_groups=mesh['expert'=64,'tensor'=16] {'expert'}, dimensions={0} | all-to-all | bytes 786432 | tf_op jit(solution)/shard_map/all_to_all | solution.py:46
  52.7 0.1 reshape.121
  52.8 5.3 %collective-permute-start = (bf16[128,1536]{1,0:T(8,128)(2,1)S(1)}, bf16[128,1536]{1,0:T(8,128)(2,1)S(1)}, u32[]{:S(2)}, u32[]{:S(2)}) collective-permute-start(bf16[128,1536]{1,0:T(8,128)(2,1)S(1)} %reshape.121), channel_id=1, source_target_pairs={{0,1},{1,0},{2,3},{3,2},{4,5},{5,4},{6,7},{7,6},{8,9},{9,8},{10,11... | collective-permute-start | bytes 1179656 | tf_op jit(solution)/shard_map/ppermute | solution.py:48
  58.1 0.7 fusion.34
  58.8 0.2 convert_reduce_fusion.1
  59.0 0.4 collective-permute-done
  59.5 0.3 fusion.2
  59.8 0.8 copy-done.3
  60.7 0.5 multiply_reduce_fusion
  61.1 0.2 copy-done.2
  61.6 0.3 convolution_convert_fusion.3
  61.9 2.3 %collective-permute-start.1 = (bf16[128,768]{1,0:T(8,128)(2,1)S(1)}, bf16[128,768]{1,0:T(8,128)(2,1)S(1)}, u32[]{:S(2)}, u32[]{:S(2)}) collective-permute-start(bf16[128,768]{1,0:T(8,128)(2,1)S(1)} %convolution_convert_fusion.3), channel_id=1, source_target_pairs={{0,1},{1,0},{2,3},{3,2},{4,5},{5,4},{6,7},{7,6},{8,9},{9,8},{10,11... | collective-permute-start | bytes 589832 | tf_op jit(solution)/shard_map/ppermute | solution.py:72
  64.2 1.0 collective-permute-done.1
  65.2 0.3 add_convert_fusion
  65.5 0.8 reshape.122
  66.3 5.4 %all-to-all-start.1 = ((bf16[64,2,768]{2,1,0:T(2,128)(2,1)}), bf16[64,2,768]{2,1,0:T(2,128)(2,1)S(1)}, u32[]{:S(2)}, u32[]{:S(2)}) async-start(bf16[64,2,768]{2,1,0:T(2,128)(2,1)} %reshape.122), calls=%async_computation.1 | async-start | bytes 393216 | tf_op jit(solution)/shard_map/all_to_all | solution.py:74
  72.0 17.3 %all-to-all-done.1 = bf16[64,2,768]{2,1,0:T(2,128)(2,1)S(1)} async-done(((bf16[64,2,768]{2,1,0:T(2,128)(2,1)}), bf16[64,2,768]{2,1,0:T(2,128)(2,1)S(1)}, u32[]{:S(2)}, u32[]{:S(2)}) %all-to-all-start.1) | async-done | bytes 196640 | tf_op jit(solution)/shard_map/all_to_all | solution.py:74
  89.4 0.3 convolution_convert_fusion.4
  89.7 0.7 pad_maximum_fusion.6
  90.4 10.4 %all-to-all-start.2 = ((bf16[16,4,896]{2,1,0:T(4,128)(2,1)}), bf16[16,4,896]{2,1,0:T(4,128)(2,1)S(1)}, u32[]{:S(2)}, u32[]{:S(2)}) async-start(bf16[16,4,896]{2,1,0:T(4,128)(2,1)} %pad_maximum_fusion.6), calls=%async_computation.2 | async-start | bytes 229376 | tf_op jit(solution)/shard_map/all_to_all | solution.py:92
  100.8 1.3 %fusion = bf16[1,1536,256]{2,1,0:T(8,128)(2,1)} fusion(bf16[128,256]{1,0:T(8,128)(2,1)S(1)} %fusion.24, bf16[128,768]{1,0:T(8,128)(2,1)S(1)} %get-tuple-element.43, bf16[128,768]{1,0:T(8,128)(2,1)S(1)} %get-tuple-element.34), kind=kOutput, calls=%fused_computation.2 | convolution fusion | flops 101842944 | bytes 1245184 | tf_op jit(solution)/shard_map/dot_general | solution.py:8
  102.1 1.3 %fusion.1 = bf16[1,256,1536]{2,1,0:T(8,128)(2,1)} fusion(f32[128]{0:T(128)S(1)} %get-tuple-element.30, bf16[128,768]{1,0:T(8,128)(2,1)S(1)} %get-tuple-element.42, bf16[128,768]{1,0:T(8,128)(2,1)S(1)} %get-tuple-element.35, f32[128,256]{1,0:T(8,128)S(1)} %fusion.2), kind=kOutput, calls=%fused_computation.3 | convolution fusion | flops 102531072 | bytes 1311232 | tf_op jit(solution)/shard_map/dot_general | solution.py:8
  103.4 6.2 %all-to-all-done.2 = bf16[16,4,896]{2,1,0:T(4,128)(2,1)S(1)} async-done(((bf16[16,4,896]{2,1,0:T(4,128)(2,1)}), bf16[16,4,896]{2,1,0:T(4,128)(2,1)S(1)}, u32[]{:S(2)}, u32[]{:S(2)}) %all-to-all-start.2) | async-done | bytes 114720 | tf_op jit(solution)/shard_map/all_to_all | solution.py:92
  109.7 0.5 slice_reduce_fusion
  110.4 0.6 copy.28
  (29 shorter events, 1.2 us)
Async XLA Ops:
  0.6 58.9 %copy-start = (bf16[1,1536,256]{2,1,0:T(8,128)(2,1)S(1)}, bf16[1,1536,256]{2,1,0:T(8,128)(2,1)}, u32[]{:S(2)}) copy-start(bf16[1,1536,256]{2,1,0:T(8,128)(2,1)} %param.16) | copy-start | bytes 2359300
  52.8 6.6 %collective-permute-start = (bf16[128,1536]{1,0:T(8,128)(2,1)S(1)}, bf16[128,1536]{1,0:T(8,128)(2,1)S(1)}, u32[]{:S(2)}, u32[]{:S(2)}) collective-permute-start(bf16[128,1536]{1,0:T(8,128)(2,1)S(1)} %reshape.121), channel_id=1, source_target_pairs={{0,1},{1,0},{2,3},{3,2},{4,5},{5,4},{6,7},{7,6},{8,9},{9,8},{10,11... | collective-permute-start | bytes 1179656 | tf_op jit(solution)/shard_map/ppermute | solution.py:48
  59.5 1.1 %copy-start.3 = (bf16[1,256,1536]{2,1,0:T(8,128)(2,1)S(1)}, bf16[1,256,1536]{2,1,0:T(8,128)(2,1)}, u32[]{:S(2)}) copy-start(bf16[1,256,1536]{2,1,0:T(8,128)(2,1)} %param.17) | copy-start | bytes 2359300
  60.7 0.7 copy-start.2
  61.9 3.3 %collective-permute-start.1 = (bf16[128,768]{1,0:T(8,128)(2,1)S(1)}, bf16[128,768]{1,0:T(8,128)(2,1)S(1)}, u32[]{:S(2)}, u32[]{:S(2)}) collective-permute-start(bf16[128,768]{1,0:T(8,128)(2,1)S(1)} %convolution_convert_fusion.3), channel_id=1, source_target_pairs={{0,1},{1,0},{2,3},{3,2},{4,5},{5,4},{6,7},{7,6},{8,9},{9,8},{10,11... | collective-permute-start | bytes 589832 | tf_op jit(solution)/shard_map/ppermute | solution.py:72
  64.2 7.5 %copy-start.1 = (s32[64,12]{0,1:T(8,128)S(1)}, s32[64,12]{0,1:T(8,128)}, u32[]{:S(2)}) copy-start(s32[64,12]{0,1:T(8,128)} %param.12) | copy-start | bytes 9220
  66.3 23.0 %all-to-all-start.1 = ((bf16[64,2,768]{2,1,0:T(2,128)(2,1)}), bf16[64,2,768]{2,1,0:T(2,128)(2,1)S(1)}, u32[]{:S(2)}, u32[]{:S(2)}) async-start(bf16[64,2,768]{2,1,0:T(2,128)(2,1)} %reshape.122), calls=%async_computation.1 | async-start | bytes 393216 | tf_op jit(solution)/shard_map/all_to_all | solution.py:74
  90.4 19.2 %all-to-all-start.2 = ((bf16[16,4,896]{2,1,0:T(4,128)(2,1)}), bf16[16,4,896]{2,1,0:T(4,128)(2,1)S(1)}, u32[]{:S(2)}, u32[]{:S(2)}) async-start(bf16[16,4,896]{2,1,0:T(4,128)(2,1)} %pad_maximum_fusion.6), calls=%async_computation.2 | async-start | bytes 229376 | tf_op jit(solution)/shard_map/all_to_all | solution.py:92

commit v2 on v1

--- a/solution.py
+++ b/solution.py
@@ -1,6 +1,8 @@
 import jax
 import jax.numpy as jnp
 from jax import lax
+from jax.experimental import pallas as pl
+from jax.experimental.pallas import tpu as pltpu
 from jax.sharding import PartitionSpec as P
 
 
@@ -18,45 +20,148 @@
     return widened.reshape(row_count, block_count * 128)
 
 
+def place_of(expert, expert_count):
+    planes = expert_count // 4
+    plane, turned, bit = expert // 4, 0, 1
+    while bit < planes:
+        turned = turned * 2 + plane // bit % 2
+        bit *= 2
+    return turned * 4 + expert % 4
+
+
+SPLIT = 4
+
+
+def iota(shape, dim):
+    return lax.broadcasted_iota(jnp.int32, shape, dim)
+
+
+def one_hot(hit):
+    return hit.astype(jnp.float32).astype(jnp.bfloat16)
+
+
+def pick_kernel(
+    slots_hbm, tokens_hbm, exponents_hbm, grads_hbm, sent_ref, pick_ref, slots, tokens, exponents, grads, done
+):
+    expert_count, slot_count = slots.shape
+    tok_count, part = tokens.shape
+    me = lax.axis_index("expert")
+    quarter = lax.axis_index("tensor") % SPLIT
+    columns = pl.ds(pl.multiple_of(quarter * part, part), part)
+    copies = [
+        pltpu.make_async_copy(source, target, done.at[index])
+        for index, (source, target) in enumerate(
+            [
+                (slots_hbm, slots),
+                (exponents_hbm, exponents),
+                (tokens_hbm.at[:, columns], tokens),
+                (grads_hbm.at[:, columns], grads),
+            ]
+        )
+    ]
+    for copy in copies:
+        copy.start()
+    row = iota((slot_count, slot_count), 0)
+    source = place_of(row // 2, expert_count) + (row % 2) * expert_count
+    spread = one_hot(source == iota((slot_count, slot_count), 1))
+    token = iota((expert_count, tok_count), 1)
+    blocks = exponents.shape[0]
+    lanes = iota((blocks, part), 1) // 128 + quarter * (part // 128)
+    widen = one_hot(lanes == iota((blocks, part), 0))
+    copies[0].wait()
+    local_index = slots[...] - me * tok_count
+    from_here = (local_index >= 0) & (local_index < tok_count)
+    lower = jnp.min(jnp.where(from_here, local_index, tok_count), axis=1, keepdims=True)
+    upper = jnp.max(jnp.where(from_here, local_index, -1), axis=1, keepdims=True)
+    hits = jnp.concatenate([one_hot(token == lower), one_hot(token == upper)], axis=0)
+    pick = contract(spread, hits, 1, 0).astype(jnp.bfloat16)
+    pick_ref[...] = pick
+    copies[1].wait()
+    factors = jnp.exp2(exponents[...].astype(jnp.float32)).astype(jnp.bfloat16)
+    scales = contract(factors, widen, 0, 0)
+    copies[2].wait()
+    scaled = (tokens[...].astype(jnp.float32) * scales).astype(jnp.bfloat16)
+    sent_ref[:, :, :part] = contract(pick, scaled, 1, 0).reshape(expert_count, 2, part).astype(jnp.bfloat16)
+    copies[3].wait()
+    sent_ref[:, :, part:] = contract(pick, grads[...], 1, 0).reshape(expert_count, 2, part).astype(jnp.bfloat16)
+
+
+def pick_rows(slots, tokens, exponents, out_grad):
+    expert_count, slot_count = slots.shape
+    tok_count, width = tokens.shape
+    part = width // SPLIT
+    anywhere = pl.BlockSpec(memory_space=pl.ANY)
+    vmem = pl.BlockSpec(memory_space=pltpu.VMEM)
+    return pl.pallas_call(
+        pick_kernel,
+        in_specs=[anywhere] * 4,
+        out_specs=[vmem, vmem],
+        out_shape=[
+            jax.ShapeDtypeStruct((expert_count, 2, 2 * part), jnp.bfloat16),
+            pltpu.VMEM((slot_count, tok_count), jnp.bfloat16),
+        ],
+        scratch_shapes=[
+            pltpu.VMEM(slots.shape, jnp.int32),
+            pltpu.VMEM((tok_count, part), jnp.bfloat16),
+            pltpu.VMEM(exponents.shape[::-1], jnp.int32),
+            pltpu.VMEM((tok_count, part), jnp.bfloat16),
+            pltpu.SemaphoreType.DMA((4,)),
+        ],
+        name="pick_rows",
+    )(slots, tokens, exponents.T, out_grad)
+
+
+def hold_kernel(source, target, done):
+    copy = pltpu.make_async_copy(source, target, done)
+    copy.start()
+    copy.wait()
+
+
+def hold(array):
+    return pl.pallas_call(
+        hold_kernel,
+        in_specs=[pl.BlockSpec(memory_space=pl.ANY)],
+        out_specs=pl.BlockSpec(memory_space=pltpu.VMEM),
+        out_shape=pltpu.VMEM(array.shape, array.dtype),
+        scratch_shapes=[pltpu.SemaphoreType.DMA(())],
+        name="hold",
+    )(array)
+
+
 def local(tokens, exponents, out_grad, slots, gates, w_in, w_out):
     expert_count = lax.axis_size("expert")
     tensor_count = lax.axis_size("tensor")
     my_expert = lax.axis_index("expert")
     my_tensor = lax.axis_index("tensor")
     core = my_tensor % 2
-    swap = [(index, index ^ 1) for index in range(tensor_count)]
+    chips = [[index, index + 1] for index in range(0, tensor_count, 2)]
+    teams = [list(range(index, index + SPLIT)) for index in range(0, tensor_count, SPLIT)]
+    order = [[place_of(index, expert_count) for index in range(expert_count)]]
     tok_count, width = tokens.shape
     half = width // 2
-    half_blocks = exponents.shape[1] // 2
+    part = width // SPLIT
     slot_count = slots.shape[1]
 
-    local_index = slots % tok_count
-    from_here = slots // tok_count == my_expert
-    lower = jnp.min(jnp.where(from_here, local_index, tok_count), axis=1)
-    upper = jnp.max(jnp.where(from_here, local_index, -1), axis=1)
-    picked = jnp.stack([lower, upper], axis=1).reshape(slot_count)
-    pick = (picked[:, None] == jnp.arange(tok_count)[None, :]).astype(jnp.bfloat16)
-
-    scaled = apply_scales(
-        lax.dynamic_slice_in_dim(tokens, core * half, half, 1),
-        lax.dynamic_slice_in_dim(exponents, core * half_blocks, half_blocks, 1),
-    ).astype(jnp.bfloat16)
-    both = jnp.concatenate([scaled, lax.dynamic_slice_in_dim(out_grad, core * half, half, 1)], axis=1)
-    sent = contract(pick, both, 1, 0).astype(jnp.bfloat16).reshape(expert_count, 2, width)
-    mine = lax.all_to_all(sent, "expert", split_axis=0, concat_axis=0, tiled=True)
-    mine = mine.reshape(slot_count, width)
-    other = lax.ppermute(mine, "tensor", swap)
-    first = jnp.where(core == 0, mine, other)
-    second = jnp.where(core == 0, other, mine)
-    slot_rows = jnp.concatenate([first[:, :half], second[:, :half]], axis=1)
-    slot_grads = jnp.concatenate([first[:, half:], second[:, half:]], axis=1)
-
+    def exchange(rows):
+        chunks = rows.reshape(expert_count, 2, rows.shape[1])
+        return lax.all_to_all(
+            chunks, "expert", split_axis=0, concat_axis=0, axis_index_groups=order, tiled=True
+        ).reshape(rows.shape)
+
+    sent, pick = pick_rows(slots, tokens, exponents, out_grad)
+    mine = exchange(sent.reshape(slot_count, 2 * part))
     my_slots = lax.dynamic_index_in_dim(slots, my_expert, 0, keepdims=False)
     rank = jnp.sum((my_slots[:, None] > my_slots[None, :]).astype(jnp.int32), axis=1)
-    placed = rank[None, :] == jnp.arange(slot_count)[:, None]
+    place = place_of(rank // 2, expert_count) * 2 + rank % 2
+    placed = place[None, :] == jnp.arange(slot_count)[:, None]
     gate_row = jnp.sum(jnp.where(placed, gates, 0.0), axis=1)
+    weight_out = hold(w_out[0])
+    mine, gate_row, weight_out = lax.optimization_barrier((mine, gate_row, weight_out))
+    joined = lax.all_gather(mine, "tensor", axis_index_groups=teams, axis=0)
+    slot_rows = jnp.concatenate([joined[index, :, :part] for index in range(SPLIT)], axis=1)
+    slot_grads = jnp.concatenate([joined[index, :, part:] for index in range(SPLIT)], axis=1)
+
     weight_in = w_in[0]
-    weight_out = w_out[0]
     preact = jnp.dot(slot_rows, weight_in, preferred_element_type=jnp.float32)
     hidden_full, backward = jax.vjp(jax.nn.gelu, preact)
     hidden = hidden_full.astype(jnp.bfloat16)
@@ -69,14 +174,13 @@
     keep_weight = lax.dynamic_slice_in_dim(weight_in, core * half, half, 0)
     give_weight = lax.dynamic_slice_in_dim(weight_in, (1 - core) * half, half, 0)
     given = contract(dpre, give_weight, 1, 1).astype(jnp.bfloat16)
-    taken = lax.ppermute(given, "tensor", swap)
+    both = lax.all_gather(given, "tensor", axis_index_groups=chips, axis=0)
+    taken = lax.dynamic_index_in_dim(both, 1 - core, 0, keepdims=False)
     chip_back = (contract(dpre, keep_weight, 1, 1) + taken.astype(jnp.float32)).astype(jnp.bfloat16)
-    came_back = lax.all_to_all(
-        chip_back.reshape(expert_count, 2, half), "expert", split_axis=0, concat_axis=0, tiled=True
-    )
+    came_back = exchange(chip_back)
     out_weight_grad = contract(hidden, gated_grads, 0, 0).astype(jnp.bfloat16)
     in_weight_grad = contract(slot_rows, dpre, 0, 0).astype(jnp.bfloat16)
-    token_sums = contract(pick, came_back.reshape(slot_count, half), 0, 0).astype(jnp.bfloat16)
+    token_sums = contract(pick, came_back, 0, 0).astype(jnp.bfloat16)
 
     share = tok_count // tensor_count
     gate_high = gate_part.astype(jnp.bfloat16)

time: 112 us -> 104 us (0.929)
  blocking collectives: 47.5 us -> 14.1 us
  waiting for transfers between devices: 25 us -> 40.5 us
  starting transfers between devices: 23.4 us -> 35.6 us
  Pallas kernels: 0 us -> 3.68 us
  other arithmetic: 4.5 us -> 1.79 us
  local copies, waits for them, and re-layouts: 5.18 us -> 2.6 us
    all_to_all x1 -> x0, blocking collectives: 47.5 us -> none  [local(): lax.all_to_all(sent, 'expert', split_axis=0, concat_axis=0, tiled=True)]
    all_to_all x1 -> x2, starting transfers between devices: 5.44 us -> 27.4 us  [exchange(): lax.all_to_all(chunks, 'expert', split_axis=0, concat_axis=0, axis_index_...]
    all_to_all x1 -> x2, waiting for transfers between devices: 17.3 us -> 34.3 us  [exchange(): lax.all_to_all(chunks, 'expert', split_axis=0, concat_axis=0, axis_index_...]
    all_gather x0 -> x2, blocking collectives: none -> 14.1 us  [the longest x1 12 us: local(): joined = lax.all_gather(mine, 'tensor', axis_index_groups=teams, axis=0)]
    ppermute x2 -> x0, starting transfers between devices: 7.55 us -> none  [the longest x1 5.27 us: local(): other = lax.ppermute(mine, 'tensor', swap)]
    pallas_call x0 -> x2, Pallas kernels: none -> 3.68 us  [the longest x1 2.53 us: pick_rows(): pl.pallas_call(pick_kernel, in_specs=[anywhere] * 4, out_specs=[vmem, vme...]
    all_to_all x1, starting transfers between devices: 10.4 us -> 8.18 us  [local(): lax.all_to_all(packed, 'tensor', split_axis=0, concat_axis=0, tiled=True)]
    ppermute x2 -> x0, waiting for transfers between devices: 1.47 us -> none  [the longest x1 1.03 us: local(): taken = lax.ppermute(given, 'tensor', swap)]
  transfers between devices with their start and end apart: 4 -> 3, of which waited for: 4 -> 3; matrix products, arithmetic and copies ran while one was open for 3% -> 4% of each run, Pallas kernels for 0% -> 1%
where the time goes in v2:
time: 104 us; the launch traced here: 103 us
  waiting for transfers between devices  40.5 us (39%)
  starting transfers between devices  35.6 us (34%)
  blocking collectives  14.1 us (14%)
  matrix products  4.18 us (4%)
  Pallas kernels  3.68 us (4%)
  local copies, waits for them, and re-layouts  2.6 us (2%)
  other arithmetic  1.79 us (2%)
    all_to_all x2, waiting for transfers between devices, exchange(): lax.all_to_all(chunks, 'expert', split_axis=0, concat_axis=0, axis_index_...  34.3 us
    all_to_all x2, starting transfers between devices, exchange(): lax.all_to_all(chunks, 'expert', split_axis=0, concat_axis=0, axis_index_...  27.4 us
    all_gather x1, blocking collectives, local(): joined = lax.all_gather(mine, 'tensor', axis_index_groups=teams, axis=0)  12 us
    all_to_all x1, starting transfers between devices, local(): lax.all_to_all(packed, 'tensor', split_axis=0, concat_axis=0, tiled=True)  8.18 us
    all_to_all x1, waiting for transfers between devices, local(): lax.all_to_all(packed, 'tensor', split_axis=0, concat_axis=0, tiled=True)  6.23 us
    dot_general x6, matrix products, contract(): lax.dot_general(left, right, (((left_dim,), (right_dim,)), ((), ())), pre...  3.75 us
    pallas_call x1, Pallas kernels, pick_rows(): pl.pallas_call(pick_kernel, in_specs=[anywhere] * 4, out_specs=[vmem, vme...  2.53 us
    all_gather x1, blocking collectives, local(): both = lax.all_gather(given, 'tensor', axis_index_groups=chips, axis=0)  2.09 us
  transfers between devices with their start and end apart: 3, of which 3 were waited for; matrix products, arithmetic and copies ran while one was open for 4% of the time, Pallas kernels for 1%

profile of v2, /device:TPU:1, one launch (start us, length us, event | category | flops | bytes accessed | tf_op | source)
XLA Modules:
  0.0 103.3 jit_solution(16153285625081333560)
XLA Ops:
  0.6 2.5 %pick_rows.1 = (bf16[64,2,768]{2,1,0:T(2,128)(2,1)}, bf16[128,64]{1,0:T(8,128)(2,1)S(1)}) custom-call(s32[64,128]{1,0:T(8,128)} %slots_hbm.1, bf16[64,1536]{1,0:T(8,128)(2,1)} %tokens_hbm.1, s32[12,64]{1,0:T(8,128)} %bitcast.66, bf16[64,1536]{1,0:T(8,128)(2,1)} %grads_hbm.1), custom_call_target="tpu_custom_call" | custom-call | tf_op jit(solution)/shard_map/pick_rows/pallas_call | solution.py:95
  3.2 22.8 %all-to-all-start = ((bf16[64,2,768]{2,1,0:T(2,128)(2,1)}), bf16[64,2,768]{2,1,0:T(2,128)(2,1)S(1)}, u32[]{:S(2)}, u32[]{:S(2)}) async-start(bf16[64,2,768]{2,1,0:T(2,128)(2,1)} %get-tuple-element.34), calls=%async_computation | async-start | bytes 393216 | tf_op jit(solution)/shard_map/all_to_all | solution.py:147
  26.0 1.2 %hold.1 = bf16[256,1536]{1,0:T(8,128)(2,1)S(1)} custom-call(bf16[256,1536]{1,0:T(8,128)(2,1)} %bitcast.64), custom_call_target="tpu_custom_call" | custom-call | tf_op jit(solution)/shard_map/hold/pallas_call | solution.py:121
  27.2 0.1 constant_dynamic-slice_fusion
  27.3 0.1 copy.15
  27.4 0.7 fusion.27
  28.1 0.2 convert_reduce_fusion.1
  28.3 0.1 select_reduce_fusion.1
  28.4 15.3 %all-to-all-done = bf16[64,2,768]{2,1,0:T(2,128)(2,1)S(1)} async-done(((bf16[64,2,768]{2,1,0:T(2,128)(2,1)}), bf16[64,2,768]{2,1,0:T(2,128)(2,1)S(1)}, u32[]{:S(2)}, u32[]{:S(2)}) %all-to-all-start) | async-done | bytes 196640 | tf_op jit(solution)/shard_map/all_to_all | solution.py:147
  43.7 0.1 reshape.256
  43.8 12.0 %all-gather = bf16[512,768]{1,0:T(8,128)(2,1)S(1)} all-gather(bf16[128,768]{1,0:T(8,128)(2,1)S(1)} %reshape.256), channel_id=2, replica_groups={{0,1,2,3},{4,5,6,7},{8,9,10,11},{12,13,14,15},{16,17,18,19},{20,21,22,2..., dimensions={0}, use_global_device_ids=true | all-gather | bytes 983040 | tf_op jit(solution)/shard_map/all_gather | solution.py:160
  55.8 0.1 slice_bitcast_fusion.3
  55.9 0.4 fusion.17
  56.3 0.4 fusion.16
  56.8 0.3 convolution_convert_fusion.2
  57.1 2.1 %all-gather.1 = bf16[256,768]{1,0:T(8,128)(2,1)S(1)} all-gather(bf16[128,768]{1,0:T(8,128)(2,1)S(1)} %convolution_convert_fusion.2), channel_id=3, replica_groups={{0,1},{2,3},{4,5},{6,7},{8,9},{10,11},{12,13},{14,15},{16,17},{18,19},{..., dimensions={0}, use_global_device_ids=true | all-gather | bytes 589824 | tf_op jit(solution)/shard_map/all_gather | solution.py:177
  59.2 0.3 fusion.2
  59.4 0.8 reshape.257
  60.2 4.6 %all-to-all-start.1 = ((bf16[64,2,768]{2,1,0:T(2,128)(2,1)}), bf16[64,2,768]{2,1,0:T(2,128)(2,1)S(1)}, u32[]{:S(2)}, u32[]{:S(2)}) async-start(bf16[64,2,768]{2,1,0:T(2,128)(2,1)} %reshape.257), calls=%async_computation.1 | async-start | bytes 393216 | tf_op jit(solution)/shard_map/all_to_all | solution.py:147
  64.8 0.1 select_reduce_fusion
  65.0 19.0 %all-to-all-done.1 = bf16[64,2,768]{2,1,0:T(2,128)(2,1)S(1)} async-done(((bf16[64,2,768]{2,1,0:T(2,128)(2,1)}), bf16[64,2,768]{2,1,0:T(2,128)(2,1)S(1)}, u32[]{:S(2)}, u32[]{:S(2)}) %all-to-all-start.1) | async-done | bytes 196640 | tf_op jit(solution)/shard_map/all_to_all | solution.py:147
  84.0 0.1 reshape.258
  84.1 0.2 convolution_convert_fusion.3
  84.3 0.7 pad_maximum_fusion.2
  85.0 8.2 %all-to-all-start.2 = ((bf16[16,4,896]{2,1,0:T(4,128)(2,1)}), bf16[16,4,896]{2,1,0:T(4,128)(2,1)S(1)}, u32[]{:S(2)}, u32[]{:S(2)}) async-start(bf16[16,4,896]{2,1,0:T(4,128)(2,1)} %pad_maximum_fusion.2), calls=%async_computation.2 | async-start | bytes 229376 | tf_op jit(solution)/shard_map/all_to_all | solution.py:196
  93.2 1.3 %fusion = bf16[1,1536,256]{2,1,0:T(8,128)(2,1)} fusion(bf16[128,256]{1,0:T(8,128)(2,1)S(1)} %get-tuple-element.46, bf16[128,384]{1,0:T(8,128)(2,1)S(1)} %get-tuple-element.39, bf16[128,384]{1,0:T(8,128)(2,1)S(1)} %get-tuple-element.40, bf16[128,384]{1,0:T(8,128)(2,1)S(1)} %get-tuple-element.41, bf16[128,384]{1,0:T(8,128)(2,1)S(1)} %get-tuple-element.38), kind=kOutput, calls=%fused_computation.2 | convolution fusion | flops 102629376 | bytes 1245184 | tf_op jit(solution)/shard_map/dot_general | solution.py:10
  94.5 1.3 %fusion.1 = bf16[1,256,1536]{2,1,0:T(8,128)(2,1)} fusion(f32[128]{0:T(128)S(1)} %select_reduce_fusion.1, bf16[128,384]{1,0:T(8,128)(2,1)S(1)} %get-tuple-element.42, bf16[128,384]{1,0:T(8,128)(2,1)S(1)} %get-tuple-element.43, bf16[128,384]{1,0:T(8,128)(2,1)S(1)} %get-tuple-element.44, bf16[128,384]{1,0:T(8,128)(2,1)S(1)} %get-tuple-element.45, ...), kind=kOutput, calls=%fused_computation.3 | convolution fusion | flops 103317504 | bytes 1311232 | tf_op jit(solution)/shard_map/dot_general | solution.py:10
  95.8 6.2 %all-to-all-done.2 = bf16[16,4,896]{2,1,0:T(4,128)(2,1)S(1)} async-done(((bf16[16,4,896]{2,1,0:T(4,128)(2,1)}), bf16[16,4,896]{2,1,0:T(4,128)(2,1)S(1)}, u32[]{:S(2)}, u32[]{:S(2)}) %all-to-all-start.2) | async-done | bytes 114720 | tf_op jit(solution)/shard_map/all_to_all | solution.py:196
  102.0 0.1 convert_reduce_fusion
  102.1 0.5 slice_reduce_fusion
  102.7 0.1 fusion.19
  102.7 0.6 copy.18
  (17 shorter events, 0.2 us)
Async XLA Ops:
  0.6 55.7 %copy-start = (bf16[1,1536,256]{2,1,0:T(8,128)(2,1)S(1)}, bf16[1,1536,256]{2,1,0:T(8,128)(2,1)}, u32[]{:S(2)}) copy-start(bf16[1,1536,256]{2,1,0:T(8,128)(2,1)} %param.16) | copy-start | bytes 2359300
  3.2 40.5 %all-to-all-start = ((bf16[64,2,768]{2,1,0:T(2,128)(2,1)}), bf16[64,2,768]{2,1,0:T(2,128)(2,1)S(1)}, u32[]{:S(2)}, u32[]{:S(2)}) async-start(bf16[64,2,768]{2,1,0:T(2,128)(2,1)} %get-tuple-element.34), calls=%async_computation | async-start | bytes 393216 | tf_op jit(solution)/shard_map/all_to_all | solution.py:147
  26.0 1.2 %copy-start.1 = (s32[64,12]{0,1:T(8,128)S(1)}, s32[64,12]{0,1:T(8,128)}, u32[]{:S(2)}) copy-start(s32[64,12]{0,1:T(8,128)} %param.12) | copy-start | bytes 9220
  26.0 2.3 %copy-start.2 = (f32[1,128]{1,0:T(1,128)S(1)}, f32[1,128]{1,0:T(1,128)}, u32[]{:S(2)}) copy-start(f32[1,128]{1,0:T(1,128)} %param.15) | copy-start | bytes 1540
  60.2 23.8 %all-to-all-start.1 = ((bf16[64,2,768]{2,1,0:T(2,128)(2,1)}), bf16[64,2,768]{2,1,0:T(2,128)(2,1)S(1)}, u32[]{:S(2)}, u32[]{:S(2)}) async-start(bf16[64,2,768]{2,1,0:T(2,128)(2,1)} %reshape.257), calls=%async_computation.1 | async-start | bytes 393216 | tf_op jit(solution)/shard_map/all_to_all | solution.py:147
  85.0 17.0 %all-to-all-start.2 = ((bf16[16,4,896]{2,1,0:T(4,128)(2,1)}), bf16[16,4,896]{2,1,0:T(4,128)(2,1)S(1)}, u32[]{:S(2)}, u32[]{:S(2)}) async-start(bf16[16,4,896]{2,1,0:T(4,128)(2,1)} %pad_maximum_fusion.2), calls=%async_computation.2 | async-start | bytes 229376 | tf_op jit(solution)/shard_map/all_to_all | solution.py:196

commit v3 on v2

--- a/solution.py
+++ b/solution.py
@@ -10,14 +10,6 @@
     return lax.dot_general(
         left, right, (((left_dim,), (right_dim,)), ((), ())), preferred_element_type=jnp.float32
     )
-
-
-def apply_scales(values, exponents):
-    row_count = values.shape[0]
-    block_count = exponents.shape[1]
-    factors = jnp.exp2(exponents.astype(jnp.float32))
-    widened = values.astype(jnp.float32).reshape(row_count, block_count, 128) * factors[:, :, None]
-    return widened.reshape(row_count, block_count * 128)
 
 
 def place_of(expert, expert_count):
@@ -81,9 +73,9 @@
     scales = contract(factors, widen, 0, 0)
     copies[2].wait()
     scaled = (tokens[...].astype(jnp.float32) * scales).astype(jnp.bfloat16)
-    sent_ref[:, :, :part] = contract(pick, scaled, 1, 0).reshape(expert_count, 2, part).astype(jnp.bfloat16)
+    sent_ref[:, :, :part] = contract(pick, scaled, 1, 0).astype(jnp.bfloat16).reshape(expert_count, 2, part)
     copies[3].wait()
-    sent_ref[:, :, part:] = contract(pick, grads[...], 1, 0).reshape(expert_count, 2, part).astype(jnp.bfloat16)
+    sent_ref[:, :, part:] = contract(pick, grads[...], 1, 0).astype(jnp.bfloat16).reshape(expert_count, 2, part)
 
 
 def pick_rows(slots, tokens, exponents, out_grad):
@@ -180,6 +172,9 @@
     came_back = exchange(chip_back)
     out_weight_grad = contract(hidden, gated_grads, 0, 0).astype(jnp.bfloat16)
     in_weight_grad = contract(slot_rows, dpre, 0, 0).astype(jnp.bfloat16)
+    came_back, out_weight_grad, in_weight_grad = lax.optimization_barrier(
+        (came_back, out_weight_grad, in_weight_grad)
+    )
     token_sums = contract(pick, came_back, 0, 0).astype(jnp.bfloat16)
 
     share = tok_count // tensor_count
@@ -193,12 +188,14 @@
         ],
         axis=2,
     )
+    my_exponents = lax.dynamic_slice_in_dim(exponents, my_tensor * share, share, 0)
+    scales = jnp.repeat(jnp.exp2(my_exponents.astype(jnp.float32)), 128, axis=1)
+    packed, scales = lax.optimization_barrier((packed, scales))
     arrived = lax.all_to_all(packed, "tensor", split_axis=0, concat_axis=0, tiled=True)
-    summed = jnp.sum(arrived.astype(jnp.float32).reshape(tensor_count // 2, 2, share, -1), axis=0)
-    my_share = jnp.concatenate([summed[0, :, :half], summed[1, :, :half]], axis=1)
-    gate_total = jnp.sum(summed[:, :2, half:], axis=(0, 1))
-    my_scales = lax.dynamic_slice_in_dim(exponents, my_tensor * share, share, 0)
-    token_grad = apply_scales(my_share, my_scales).astype(jnp.bfloat16)
+    halves = jnp.sum(arrived.astype(jnp.float32).reshape(tensor_count // 2, 2, share, -1), axis=0)
+    gate_total = jnp.sum(halves[:, :2, half:], axis=(0, 1))
+    my_share = jnp.concatenate([halves[0, :, :half], halves[1, :, :half]], axis=1)
+    token_grad = (my_share * scales).astype(jnp.bfloat16)
     return (token_grad, in_weight_grad[None], out_weight_grad[None], gate_total[None])
 
 

time: 104 us -> 103 us (level)
  blocking collectives: 14.1 us -> 30.9 us
  waiting for transfers between devices: 40.5 us -> 31.6 us
  starting transfers between devices: 35.6 us -> 27.4 us
    all_to_all x0 -> x1, blocking collectives: none -> 16.8 us  [local(): lax.all_to_all(packed, 'tensor', split_axis=0, concat_axis=0, tiled=True)]
    all_to_all x1 -> x0, starting transfers between devices: 8.18 us -> none  [local(): lax.all_to_all(packed, 'tensor', split_axis=0, concat_axis=0, tiled=True)]
    all_to_all x1 -> x0, waiting for transfers between devices: 6.23 us -> none  [local(): lax.all_to_all(packed, 'tensor', split_axis=0, concat_axis=0, tiled=True)]
    all_to_all x2, waiting for transfers between devices: 34.3 us -> 31.6 us  [exchange(): lax.all_to_all(chunks, 'expert', split_axis=0, concat_axis=0, axis_index_...]
  transfers between devices with their start and end apart: 3 -> 2, of which waited for: 3 -> 2; matrix products, arithmetic and copies ran while one was open for 4% -> 4% of each run, Pallas kernels for 1% -> 1%
where the time goes in v3:
time: 103 us; the launch traced here: 102 us
  waiting for transfers between devices  31.6 us (31%)
  blocking collectives  30.9 us (30%)
  starting transfers between devices  27.4 us (27%)
  matrix products  4.19 us (4%)
  Pallas kernels  3.55 us (3%)
  local copies, waits for them, and re-layouts  2.06 us (2%)
  other arithmetic  1.69 us (2%)
    all_to_all x2, waiting for transfers between devices, exchange(): lax.all_to_all(chunks, 'expert', split_axis=0, concat_axis=0, axis_index_...  31.6 us
    all_to_all x2, starting transfers between devices, exchange(): lax.all_to_all(chunks, 'expert', split_axis=0, concat_axis=0, axis_index_...  27.4 us
    all_to_all x1, blocking collectives, local(): lax.all_to_all(packed, 'tensor', split_axis=0, concat_axis=0, tiled=True)  16.8 us
    all_gather x1, blocking collectives, local(): joined = lax.all_gather(mine, 'tensor', axis_index_groups=teams, axis=0)  12.1 us
    dot_general x6, matrix products, contract(): lax.dot_general(left, right, (((left_dim,), (right_dim,)), ((), ())), pre...  3.76 us
    pallas_call x1, Pallas kernels, pick_rows(): pl.pallas_call(pick_kernel, in_specs=[anywhere] * 4, out_specs=[vmem, vme...  2.4 us
    all_gather x1, blocking collectives, local(): both = lax.all_gather(given, 'tensor', axis_index_groups=chips, axis=0)  2.09 us
  transfers between devices with their start and end apart: 2, of which 2 were waited for; matrix products, arithmetic and copies ran while one was open for 4% of the time, Pallas kernels for 1%

profile of v3, /device:TPU:1, one launch (start us, length us, event | category | flops | bytes accessed | tf_op | source)
XLA Modules:
  0.0 102.3 jit_solution(14161050417438646839)
XLA Ops:
  0.6 2.4 %pick_rows.1 = (bf16[64,2,768]{2,1,0:T(2,128)(2,1)}, bf16[128,64]{1,0:T(8,128)(2,1)S(1)}) custom-call(s32[64,128]{1,0:T(8,128)} %slots_hbm.1, bf16[64,1536]{1,0:T(8,128)(2,1)} %tokens_hbm.1, s32[12,64]{1,0:T(8,128)} %bitcast.69, bf16[64,1536]{1,0:T(8,128)(2,1)} %grads_hbm.1), custom_call_target="tpu_custom_call" | custom-call | tf_op jit(solution)/shard_map/pick_rows/pallas_call | solution.py:87
  3.1 22.8 %all-to-all-start = ((bf16[64,2,768]{2,1,0:T(2,128)(2,1)}), bf16[64,2,768]{2,1,0:T(2,128)(2,1)S(1)}, u32[]{:S(2)}, u32[]{:S(2)}) async-start(bf16[64,2,768]{2,1,0:T(2,128)(2,1)} %get-tuple-element.39), calls=%async_computation | async-start | bytes 393216 | tf_op jit(solution)/shard_map/all_to_all | solution.py:139
  25.9 1.2 %hold.1 = bf16[256,1536]{1,0:T(8,128)(2,1)S(1)} custom-call(bf16[256,1536]{1,0:T(8,128)(2,1)} %bitcast.66), custom_call_target="tpu_custom_call" | custom-call | tf_op jit(solution)/shard_map/hold/pallas_call | solution.py:113
  27.1 0.1 constant_dynamic-slice_fusion
  27.1 0.1 copy.15
  27.3 0.1 broadcast_bitcast_fusion
  27.4 0.7 fusion.24
  28.1 0.2 convert_reduce_fusion.1
  28.2 0.1 fusion.23
  28.3 0.1 select_reduce_fusion.1
  28.4 15.2 %all-to-all-done = bf16[64,2,768]{2,1,0:T(2,128)(2,1)S(1)} async-done(((bf16[64,2,768]{2,1,0:T(2,128)(2,1)}), bf16[64,2,768]{2,1,0:T(2,128)(2,1)S(1)}, u32[]{:S(2)}, u32[]{:S(2)}) %all-to-all-start) | async-done | bytes 196640 | tf_op jit(solution)/shard_map/all_to_all | solution.py:139
  43.6 0.1 reshape.248
  43.7 12.1 %all-gather = bf16[512,768]{1,0:T(8,128)(2,1)S(1)} all-gather(bf16[128,768]{1,0:T(8,128)(2,1)S(1)} %reshape.248), channel_id=2, replica_groups={{0,1,2,3},{4,5,6,7},{8,9,10,11},{12,13,14,15},{16,17,18,19},{20,21,22,2..., dimensions={0}, use_global_device_ids=true | all-gather | bytes 983040 | tf_op jit(solution)/shard_map/all_gather | solution.py:152
  55.7 0.1 slice_bitcast_fusion.3
  55.8 0.4 fusion.15
  56.2 0.4 fusion.14
  56.6 0.3 convolution_convert_fusion.2
  56.9 2.1 %all-gather.1 = bf16[256,768]{1,0:T(8,128)(2,1)S(1)} all-gather(bf16[128,768]{1,0:T(8,128)(2,1)S(1)} %convolution_convert_fusion.2), channel_id=3, replica_groups={{0,1},{2,3},{4,5},{6,7},{8,9},{10,11},{12,13},{14,15},{16,17},{18,19},{..., dimensions={0}, use_global_device_ids=true | all-gather | bytes 589824 | tf_op jit(solution)/shard_map/all_gather | solution.py:169
  59.0 0.3 fusion
  59.3 0.8 reshape.249
  60.1 4.6 %all-to-all-start.1 = ((bf16[64,2,768]{2,1,0:T(2,128)(2,1)}), bf16[64,2,768]{2,1,0:T(2,128)(2,1)S(1)}, u32[]{:S(2)}, u32[]{:S(2)}) async-start(bf16[64,2,768]{2,1,0:T(2,128)(2,1)} %reshape.249), calls=%async_computation.1 | async-start | bytes 393216 | tf_op jit(solution)/shard_map/all_to_all | solution.py:139
  64.7 0.1 select_reduce_fusion
  64.9 1.3 %convolution_convert_fusion = bf16[1536,256]{1,0:T(8,128)(2,1)} fusion(bf16[128,256]{1,0:T(8,128)(2,1)S(1)} %get-tuple-element.56, bf16[128,384]{1,0:T(8,128)(2,1)S(1)} %get-tuple-element.49, bf16[128,384]{1,0:T(8,128)(2,1)S(1)} %get-tuple-element.50, bf16[128,384]{1,0:T(8,128)(2,1)S(1)} %get-tuple-element.51, bf16[128,384]{1,0:T(8,128)(2,1)S(1)} %get-tuple-element.48), kind=kOutput, calls=%fused_computation | convolution fusion | flops 102629376 | bytes 1245184 | tf_op jit(solution)/shard_map/dot_general | solution.py:10
  66.1 1.3 %convolution_convert_fusion.1 = bf16[256,1536]{1,0:T(8,128)(2,1)} fusion(f32[128]{0:T(128)S(1)} %select_reduce_fusion.1, bf16[128,384]{1,0:T(8,128)(2,1)S(1)} %get-tuple-element.52, bf16[128,384]{1,0:T(8,128)(2,1)S(1)} %get-tuple-element.53, bf16[128,384]{1,0:T(8,128)(2,1)S(1)} %get-tuple-element.54, bf16[128,384]{1,0:T(8,128)(2,1)S(1)} %get-tuple-element.55, ...), kind=kOutput, calls=%fused_computation.1 | convolution fusion | flops 103317504 | bytes 1311232 | tf_op jit(solution)/shard_map/dot_general | solution.py:10
  67.5 16.4 %all-to-all-done.1 = bf16[64,2,768]{2,1,0:T(2,128)(2,1)S(1)} async-done(((bf16[64,2,768]{2,1,0:T(2,128)(2,1)}), bf16[64,2,768]{2,1,0:T(2,128)(2,1)S(1)}, u32[]{:S(2)}, u32[]{:S(2)}) %all-to-all-start.1) | async-done | bytes 196640 | tf_op jit(solution)/shard_map/all_to_all | solution.py:139
  83.9 0.1 reshape.250
  84.0 0.2 convolution_convert_fusion.3
  84.2 0.1 pad_maximum_fusion.2
  84.3 16.8 %all_to_all.15 = bf16[16,4,896]{2,1,0:T(4,128)(2,1)S(1)} all-to-all(bf16[16,4,896]{2,1,0:T(4,128)(2,1)S(1)} %pad_maximum_fusion.2), channel_id=1, replica_groups=mesh['expert'=64,'tensor'=16] {'tensor'}, dimensions={0} | all-to-all | bytes 229376 | tf_op jit(solution)/shard_map/all_to_all | solution.py:194
  101.1 0.1 convert_reduce_fusion
  101.1 0.5 slice_reduce_fusion
  101.7 0.6 fusion.16
  (15 shorter events, 0.1 us)
Async XLA Ops:
  0.6 55.6 %copy-start = (bf16[1,1536,256]{2,1,0:T(8,128)(2,1)S(1)}, bf16[1,1536,256]{2,1,0:T(8,128)(2,1)}, u32[]{:S(2)}) copy-start(bf16[1,1536,256]{2,1,0:T(8,128)(2,1)} %param.16) | copy-start | bytes 2359300
  3.1 40.5 %all-to-all-start = ((bf16[64,2,768]{2,1,0:T(2,128)(2,1)}), bf16[64,2,768]{2,1,0:T(2,128)(2,1)S(1)}, u32[]{:S(2)}, u32[]{:S(2)}) async-start(bf16[64,2,768]{2,1,0:T(2,128)(2,1)} %get-tuple-element.39), calls=%async_computation | async-start | bytes 393216 | tf_op jit(solution)/shard_map/all_to_all | solution.py:139
  25.9 1.2 %copy-start.1 = (s32[64,12]{0,1:T(8,128)S(1)}, s32[64,12]{0,1:T(8,128)}, u32[]{:S(2)}) copy-start(s32[64,12]{0,1:T(8,128)} %param.12) | copy-start | bytes 9220
  25.9 2.4 %copy-start.2 = (f32[1,128]{1,0:T(1,128)S(1)}, f32[1,128]{1,0:T(1,128)}, u32[]{:S(2)}) copy-start(f32[1,128]{1,0:T(1,128)} %param.15) | copy-start | bytes 1540
  60.1 23.8 %all-to-all-start.1 = ((bf16[64,2,768]{2,1,0:T(2,128)(2,1)}), bf16[64,2,768]{2,1,0:T(2,128)(2,1)S(1)}, u32[]{:S(2)}, u32[]{:S(2)}) async-start(bf16[64,2,768]{2,1,0:T(2,128)(2,1)} %reshape.249), calls=%async_computation.1 | async-start | bytes 393216 | tf_op jit(solution)/shard_map/all_to_all | solution.py:139

commit v4 on v3

--- a/solution.py
+++ b/solution.py
@@ -120,6 +120,57 @@
     )(array)
 
 
+def in_vmem(*arrays):
+    return [pltpu.with_memory_space_constraint(array, pltpu.VMEM) for array in arrays]
+
+
+def back_kernel(dpre_ref, weight_ref, other_weight_ref, back_ref):
+    half = other_weight_ref.shape[1]
+    core = lax.axis_index("tensor") % 2
+    columns = pl.ds(pl.multiple_of(core * half, half), half)
+    total = contract(dpre_ref[core], weight_ref[columns, :], 1, 1)
+    total += contract(dpre_ref[1 - core], other_weight_ref[1 - core], 1, 1)
+    back_ref[...] = total.astype(jnp.bfloat16).reshape(back_ref.shape)
+
+
+def chip_sums(dpre, weight_in, other_weights):
+    slot_count, half = dpre.shape[1], other_weights.shape[1]
+    return pl.pallas_call(
+        back_kernel,
+        in_specs=[pl.BlockSpec(memory_space=pltpu.VMEM)] * 3,
+        out_specs=pl.BlockSpec(memory_space=pltpu.VMEM),
+        out_shape=jax.ShapeDtypeStruct((slot_count // 2, 2, half), jnp.bfloat16),
+        name="chip_sums",
+    )(*in_vmem(dpre, weight_in, other_weights))
+
+
+def finish_kernel(arrived_ref, scales_ref, token_grad_ref, gate_ref):
+    devices = arrived_ref.shape[0]
+    half = token_grad_ref.shape[1] // 2
+    first = arrived_ref[0].astype(jnp.float32)
+    second = arrived_ref[1].astype(jnp.float32)
+    for index in range(2, devices, 2):
+        first += arrived_ref[index].astype(jnp.float32)
+        second += arrived_ref[index + 1].astype(jnp.float32)
+    token_grad_ref[:, :half] = (first[:, :half] * scales_ref[:, :half]).astype(jnp.bfloat16)
+    token_grad_ref[:, half:] = (second[:, :half] * scales_ref[:, half:]).astype(jnp.bfloat16)
+    gates = first[:, half:] + second[:, half:]
+    gate_ref[...] = gates[0:1] + gates[1:2]
+
+
+def finish(arrived, scales, slot_count):
+    return pl.pallas_call(
+        finish_kernel,
+        in_specs=[pl.BlockSpec(memory_space=pltpu.VMEM)] * 2,
+        out_specs=[pl.BlockSpec(memory_space=pltpu.VMEM)] * 2,
+        out_shape=[
+            jax.ShapeDtypeStruct(scales.shape, jnp.bfloat16),
+            jax.ShapeDtypeStruct((1, slot_count), jnp.float32),
+        ],
+        name="finish",
+    )(*in_vmem(arrived, scales))
+
+
 def local(tokens, exponents, out_grad, slots, gates, w_in, w_out):
     expert_count = lax.axis_size("expert")
     tensor_count = lax.axis_size("tensor")
@@ -134,21 +185,24 @@
     part = width // SPLIT
     slot_count = slots.shape[1]
 
-    def exchange(rows):
-        chunks = rows.reshape(expert_count, 2, rows.shape[1])
+    def exchange(chunks):
         return lax.all_to_all(
             chunks, "expert", split_axis=0, concat_axis=0, axis_index_groups=order, tiled=True
-        ).reshape(rows.shape)
+        ).reshape(slot_count, chunks.shape[2])
 
     sent, pick = pick_rows(slots, tokens, exponents, out_grad)
-    mine = exchange(sent.reshape(slot_count, 2 * part))
+    mine = exchange(sent)
     my_slots = lax.dynamic_index_in_dim(slots, my_expert, 0, keepdims=False)
     rank = jnp.sum((my_slots[:, None] > my_slots[None, :]).astype(jnp.int32), axis=1)
     place = place_of(rank // 2, expert_count) * 2 + rank % 2
     placed = place[None, :] == jnp.arange(slot_count)[:, None]
     gate_row = jnp.sum(jnp.where(placed, gates, 0.0), axis=1)
     weight_out = hold(w_out[0])
-    mine, gate_row, weight_out = lax.optimization_barrier((mine, gate_row, weight_out))
+    give_weight = lax.dynamic_slice_in_dim(w_in[0], (1 - core) * half, half, 0)
+    other_weights = lax.all_gather(give_weight, "tensor", axis_index_groups=chips, axis=0)
+    mine, gate_row, weight_out, other_weights = lax.optimization_barrier(
+        (mine, gate_row, weight_out, other_weights)
+    )
     joined = lax.all_gather(mine, "tensor", axis_index_groups=teams, axis=0)
     slot_rows = jnp.concatenate([joined[index, :, :part] for index in range(SPLIT)], axis=1)
     slot_grads = jnp.concatenate([joined[index, :, part:] for index in range(SPLIT)], axis=1)
@@ -163,12 +217,8 @@
     dpre = backward(gate_row[:, None] * upstream)[0].astype(jnp.bfloat16)
     gated_grads = (gate_row[:, None] * slot_grads.astype(jnp.float32)).astype(jnp.bfloat16)
 
-    keep_weight = lax.dynamic_slice_in_dim(weight_in, core * half, half, 0)
-    give_weight = lax.dynamic_slice_in_dim(weight_in, (1 - core) * half, half, 0)
-    given = contract(dpre, give_weight, 1, 1).astype(jnp.bfloat16)
-    both = lax.all_gather(given, "tensor", axis_index_groups=chips, axis=0)
-    taken = lax.dynamic_index_in_dim(both, 1 - core, 0, keepdims=False)
-    chip_back = (contract(dpre, keep_weight, 1, 1) + taken.astype(jnp.float32)).astype(jnp.bfloat16)
+    both = lax.all_gather(dpre, "tensor", axis_index_groups=chips, axis=0)
+    chip_back = chip_sums(both, weight_in, other_weights)
     came_back = exchange(chip_back)
     out_weight_grad = contract(hidden, gated_grads, 0, 0).astype(jnp.bfloat16)
     in_weight_grad = contract(slot_rows, dpre, 0, 0).astype(jnp.bfloat16)
@@ -192,11 +242,8 @@
     scales = jnp.repeat(jnp.exp2(my_exponents.astype(jnp.float32)), 128, axis=1)
     packed, scales = lax.optimization_barrier((packed, scales))
     arrived = lax.all_to_all(packed, "tensor", split_axis=0, concat_axis=0, tiled=True)
-    halves = jnp.sum(arrived.astype(jnp.float32).reshape(tensor_count // 2, 2, share, -1), axis=0)
-    gate_total = jnp.sum(halves[:, :2, half:], axis=(0, 1))
-    my_share = jnp.concatenate([halves[0, :, :half], halves[1, :, :half]], axis=1)
-    token_grad = (my_share * scales).astype(jnp.bfloat16)
-    return (token_grad, in_weight_grad[None], out_weight_grad[None], gate_total[None])
+    token_grad, gate_total = finish(arrived, scales, slot_count)
+    return (token_grad, in_weight_grad[None], out_weight_grad[None], gate_total)
 
 
 def solution(mesh):

time: 103 us -> 102 us (level)
  waiting for transfers between devices: 31.6 us -> 28.5 us
  blocking collectives: 30.9 us -> 33.7 us
  Pallas kernels: 3.55 us -> 5.24 us
  other arithmetic: 1.69 us -> 0.5 us
    all_to_all x2, waiting for transfers between devices: 31.6 us -> 28.5 us  [exchange(): lax.all_to_all(chunks, 'expert', split_axis=0, concat_axis=0, axis_index_...]
    all_gather x1 -> x2, blocking collectives: 2.09 us -> 4.85 us  [the longest x1 2.95 us: local(): lax.all_gather(give_weight, 'tensor', axis_index_groups=chips, axis=0)]
    pallas_call x0 -> x2, Pallas kernels: none -> 1.7 us  [the longest x1 1.07 us: chip_sums(): pl.pallas_call(back_kernel, in_specs=[pl.BlockSpec(memory_space=pltpu.VME...]
    dot_general x6 -> x4, matrix products: 3.76 us -> 3.17 us  [contract(): lax.dot_general(left, right, (((left_dim,), (right_dim,)), ((), ())), pre...]
where the time goes in v4:
time: 102 us; the launch traced here: 101 us
  blocking collectives  33.7 us (33%)
  waiting for transfers between devices  28.5 us (28%)
  starting transfers between devices  27.4 us (27%)
  Pallas kernels  5.24 us (5%)
  matrix products  3.61 us (4%)
  local copies, waits for them, and re-layouts  1.33 us (1%)
    all_to_all x2, waiting for transfers between devices, exchange(): lax.all_to_all(chunks, 'expert', split_axis=0, concat_axis=0, axis_index_...  28.5 us
    all_to_all x2, starting transfers between devices, exchange(): lax.all_to_all(chunks, 'expert', split_axis=0, concat_axis=0, axis_index_...  27.4 us
    all_to_all x1, blocking collectives, local(): lax.all_to_all(packed, 'tensor', split_axis=0, concat_axis=0, tiled=True)  16.8 us
    all_gather x1, blocking collectives, local(): joined = lax.all_gather(mine, 'tensor', axis_index_groups=teams, axis=0)  12.1 us
    dot_general x4, matrix products, contract(): lax.dot_general(left, right, (((left_dim,), (right_dim,)), ((), ())), pre...  3.17 us
    all_gather x1, blocking collectives, local(): lax.all_gather(give_weight, 'tensor', axis_index_groups=chips, axis=0)  2.95 us
    pallas_call x1, Pallas kernels, pick_rows(): pl.pallas_call(pick_kernel, in_specs=[anywhere] * 4, out_specs=[vmem, vme...  2.33 us
  transfers between devices with their start and end apart: 2, of which 2 were waited for; matrix products, arithmetic and copies ran while one was open for 4% of the time, Pallas kernels for 1%

profile of v4, /device:TPU:1, one launch (start us, length us, event | category | flops | bytes accessed | tf_op | source)
XLA Modules:
  0.0 101.2 jit_solution(7589780730312882804)
XLA Ops:
  0.6 0.0 copy-start.1
  0.6 2.3 %pick_rows.1 = (bf16[64,2,768]{2,1,0:T(2,128)(2,1)}, bf16[128,64]{1,0:T(8,128)(2,1)S(1)}) custom-call(s32[64,128]{1,0:T(8,128)} %slots_hbm.1, bf16[64,1536]{1,0:T(8,128)(2,1)} %tokens_hbm.1, s32[12,64]{1,0:T(8,128)} %bitcast.51, bf16[64,1536]{1,0:T(8,128)(2,1)} %grads_hbm.1), custom_call_target="tpu_custom_call" | custom-call | tf_op jit(solution)/shard_map/pick_rows/pallas_call | solution.py:87
  3.0 22.8 %all-to-all-start = ((bf16[64,2,768]{2,1,0:T(2,128)(2,1)}), bf16[64,2,768]{2,1,0:T(2,128)(2,1)S(1)}, u32[]{:S(2)}, u32[]{:S(2)}) async-start(bf16[64,2,768]{2,1,0:T(2,128)(2,1)} %get-tuple-element.42), calls=%async_computation | async-start | bytes 393216 | tf_op jit(solution)/shard_map/all_to_all | solution.py:189
  25.8 0.0 copy-done.1
  25.8 0.1 constant_dynamic-slice_fusion
  25.9 0.1 copy.16
  26.0 0.1 broadcast_bitcast_fusion
  26.0 0.7 fusion.15
  26.8 1.2 %hold.1 = bf16[256,1536]{1,0:T(8,128)(2,1)S(1)} custom-call(bf16[256,1536]{1,0:T(8,128)(2,1)} %bitcast.50), custom_call_target="tpu_custom_call" | custom-call | tf_op jit(solution)/shard_map/hold/pallas_call | solution.py:113
  28.0 0.2 convert_reduce_fusion
  28.2 0.1 fusion.14
  28.2 0.0 copy-done.2
  28.2 0.1 select_reduce_fusion.1
  28.4 3.0 %all_gather.16.other_weight_ref = bf16[2,768,256]{2,1,0:T(8,128)(2,1)S(1)} all-gather(bf16[1,768,256]{2,1,0:T(8,128)(2,1)S(1)} %constant_dynamic-slice_fusion.1), channel_id=1, replica_groups={{0,1},{2,3},{4,5},{6,7},{8,9},{10,11},{12,13},{14,15},{16,17},{18,19},{..., dimensions={0}, use_global_device_ids=true | all-gather | bytes 1179648 | tf_op jit(solution)/shard_map/all_gather | solution.py:202
  31.4 12.1 %all-to-all-done = bf16[64,2,768]{2,1,0:T(2,128)(2,1)S(1)} async-done(((bf16[64,2,768]{2,1,0:T(2,128)(2,1)}), bf16[64,2,768]{2,1,0:T(2,128)(2,1)S(1)}, u32[]{:S(2)}, u32[]{:S(2)}) %all-to-all-start) | async-done | bytes 196640 | tf_op jit(solution)/shard_map/all_to_all | solution.py:189
  43.5 0.1 reshape.237
  43.6 12.1 %all-gather = bf16[512,768]{1,0:T(8,128)(2,1)S(1)} all-gather(bf16[128,768]{1,0:T(8,128)(2,1)S(1)} %reshape.237), channel_id=2, replica_groups={{0,1,2,3},{4,5,6,7},{8,9,10,11},{12,13,14,15},{16,17,18,19},{20,21,22,2..., dimensions={0}, use_global_device_ids=true | all-gather | bytes 983040 | tf_op jit(solution)/shard_map/all_gather | solution.py:206
  55.6 0.1 slice_bitcast_fusion.3
  55.7 0.4 fusion.9
  56.1 0.4 fusion.7
  56.6 1.9 %all-gather.1 = bf16[256,256]{1,0:T(8,128)(2,1)S(1)} all-gather(bf16[128,256]{1,0:T(8,128)(2,1)S(1)} %get-tuple-element.62), channel_id=3, replica_groups={{0,1},{2,3},{4,5},{6,7},{8,9},{10,11},{12,13},{14,15},{16,17},{18,19},{..., dimensions={0}, use_global_device_ids=true | all-gather | bytes 196608 | tf_op jit(solution)/shard_map/all_gather | solution.py:220
  58.5 1.1 %chip_sums.1 = bf16[64,2,768]{2,1,0:T(2,128)(2,1)} custom-call(bf16[2,128,256]{2,1,0:T(8,128)(2,1)S(1)} %bitcast.47, bf16[1536,256]{1,0:T(8,128)(2,1)S(1)} %bitcast.46, bf16[2,768,256]{2,1,0:T(8,128)(2,1)S(1)} %all_gather.16.other_weight_ref), custom_call_target="tpu_custom_call" | custom-call | tf_op jit(solution)/shard_map/chip_sums/pallas_call | solution.py:138
  59.5 4.6 %all-to-all-start.1 = ((bf16[64,2,768]{2,1,0:T(2,128)(2,1)}), bf16[64,2,768]{2,1,0:T(2,128)(2,1)S(1)}, u32[]{:S(2)}, u32[]{:S(2)}) async-start(bf16[64,2,768]{2,1,0:T(2,128)(2,1)} %chip_sums.1), calls=%async_computation.1 | async-start | bytes 393216 | tf_op jit(solution)/shard_map/all_to_all | solution.py:189
  64.2 0.1 select_reduce_fusion
  64.3 1.3 %convolution_convert_fusion = bf16[1536,256]{1,0:T(8,128)(2,1)} fusion(bf16[128,256]{1,0:T(8,128)(2,1)S(1)} %get-tuple-element.62, bf16[128,384]{1,0:T(8,128)(2,1)S(1)} %get-tuple-element.55, bf16[128,384]{1,0:T(8,128)(2,1)S(1)} %get-tuple-element.56, bf16[128,384]{1,0:T(8,128)(2,1)S(1)} %get-tuple-element.57, bf16[128,384]{1,0:T(8,128)(2,1)S(1)} %get-tuple-element.54), kind=kOutput, calls=%fused_computation | convolution fusion | flops 102629376 | bytes 1245184 | tf_op jit(solution)/shard_map/dot_general | solution.py:10
  65.6 1.3 %convolution_convert_fusion.1 = bf16[256,1536]{1,0:T(8,128)(2,1)} fusion(f32[128]{0:T(128)S(1)} %select_reduce_fusion.1, bf16[128,384]{1,0:T(8,128)(2,1)S(1)} %get-tuple-element.58, bf16[128,384]{1,0:T(8,128)(2,1)S(1)} %get-tuple-element.59, bf16[128,384]{1,0:T(8,128)(2,1)S(1)} %get-tuple-element.60, bf16[128,384]{1,0:T(8,128)(2,1)S(1)} %get-tuple-element.61, ...), kind=kOutput, calls=%fused_computation.1 | convolution fusion | flops 103317504 | bytes 1311232 | tf_op jit(solution)/shard_map/dot_general | solution.py:10
  66.9 16.4 %all-to-all-done.1 = bf16[64,2,768]{2,1,0:T(2,128)(2,1)S(1)} async-done(((bf16[64,2,768]{2,1,0:T(2,128)(2,1)}), bf16[64,2,768]{2,1,0:T(2,128)(2,1)S(1)}, u32[]{:S(2)}, u32[]{:S(2)}) %all-to-all-start.1) | async-done | bytes 196640 | tf_op jit(solution)/shard_map/all_to_all | solution.py:189
  83.3 0.1 reshape.238
  83.4 0.2 convolution_convert_fusion.2
  83.7 0.1 pad_maximum_fusion.2
  83.7 16.8 %all_to_all.15.arrived_ref = bf16[16,4,896]{2,1,0:T(4,128)(2,1)S(1)} all-to-all(bf16[16,4,896]{2,1,0:T(4,128)(2,1)S(1)} %pad_maximum_fusion.2), channel_id=1, replica_groups=mesh['expert'=64,'tensor'=16] {'tensor'}, dimensions={0} | all-to-all | bytes 229376 | tf_op jit(solution)/shard_map/all_to_all | solution.py:244
  100.5 0.6 finish.1
  (12 shorter events, 0.2 us)
Async XLA Ops:
  0.6 25.2 %copy-start.1 = (s32[64,12]{0,1:T(8,128)S(1)}, s32[64,12]{0,1:T(8,128)}, u32[]{:S(2)}) copy-start(s32[64,12]{0,1:T(8,128)} %param.12) | copy-start | bytes 9220
  3.0 40.5 %all-to-all-start = ((bf16[64,2,768]{2,1,0:T(2,128)(2,1)}), bf16[64,2,768]{2,1,0:T(2,128)(2,1)S(1)}, u32[]{:S(2)}, u32[]{:S(2)}) async-start(bf16[64,2,768]{2,1,0:T(2,128)(2,1)} %get-tuple-element.42), calls=%async_computation | async-start | bytes 393216 | tf_op jit(solution)/shard_map/all_to_all | solution.py:189
  26.8 1.5 %copy-start.2 = (f32[1,128]{1,0:T(1,128)S(1)}, f32[1,128]{1,0:T(1,128)}, u32[]{:S(2)}) copy-start(f32[1,128]{1,0:T(1,128)} %param.15) | copy-start | bytes 1540
  26.8 1.6 %copy-start = (bf16[1,1536,256]{2,1,0:T(8,128)(2,1)S(1)}, bf16[1,1536,256]{2,1,0:T(8,128)(2,1)}, u32[]{:S(2)}) copy-start(bf16[1,1536,256]{2,1,0:T(8,128)(2,1)} %param.16) | copy-start | bytes 2359300
  59.5 23.8 %all-to-all-start.1 = ((bf16[64,2,768]{2,1,0:T(2,128)(2,1)}), bf16[64,2,768]{2,1,0:T(2,128)(2,1)S(1)}, u32[]{:S(2)}, u32[]{:S(2)}) async-start(bf16[64,2,768]{2,1,0:T(2,128)(2,1)} %chip_sums.1), calls=%async_computation.1 | async-start | bytes 393216 | tf_op jit(solution)/shard_map/all_to_all | solution.py:189

commit v5 on v4

--- a/solution.py
+++ b/solution.py
@@ -32,8 +32,15 @@
     return hit.astype(jnp.float32).astype(jnp.bfloat16)
 
 
+def copy_lanes(source, target, start, count, done):
+    lanes = pl.ds(start, count)
+    copy = pltpu.make_async_copy(source.at[:, :, lanes], target.at[:, :, lanes], done)
+    copy.start()
+    return copy
+
+
 def pick_kernel(
-    slots_hbm, tokens_hbm, exponents_hbm, grads_hbm, sent_ref, pick_ref, slots, tokens, exponents, grads, done
+    slots_hbm, tokens_hbm, exponents_hbm, grads_hbm, sent_hbm, pick_ref, slots, tokens, exponents, grads, sent_ref, done
 ):
     expert_count, slot_count = slots.shape
     tok_count, part = tokens.shape
@@ -74,8 +81,12 @@
     copies[2].wait()
     scaled = (tokens[...].astype(jnp.float32) * scales).astype(jnp.bfloat16)
     sent_ref[:, :, :part] = contract(pick, scaled, 1, 0).astype(jnp.bfloat16).reshape(expert_count, 2, part)
+    rows_out = copy_lanes(sent_ref, sent_hbm, 0, part, done.at[4])
     copies[3].wait()
     sent_ref[:, :, part:] = contract(pick, grads[...], 1, 0).astype(jnp.bfloat16).reshape(expert_count, 2, part)
+    grads_out = copy_lanes(sent_ref, sent_hbm, part, part, done.at[5])
+    rows_out.wait()
+    grads_out.wait()
 
 
 def pick_rows(slots, tokens, exponents, out_grad):
@@ -87,7 +98,7 @@
     return pl.pallas_call(
         pick_kernel,
         in_specs=[anywhere] * 4,
-        out_specs=[vmem, vmem],
+        out_specs=[anywhere, vmem],
         out_shape=[
             jax.ShapeDtypeStruct((expert_count, 2, 2 * part), jnp.bfloat16),
             pltpu.VMEM((slot_count, tok_count), jnp.bfloat16),
@@ -97,7 +108,8 @@
             pltpu.VMEM((tok_count, part), jnp.bfloat16),
             pltpu.VMEM(exponents.shape[::-1], jnp.int32),
             pltpu.VMEM((tok_count, part), jnp.bfloat16),
-            pltpu.SemaphoreType.DMA((4,)),
+            pltpu.VMEM((expert_count, 2, 2 * part), jnp.bfloat16),
+            pltpu.SemaphoreType.DMA((6,)),
         ],
         name="pick_rows",
     )(slots, tokens, exponents.T, out_grad)
@@ -124,13 +136,21 @@
     return [pltpu.with_memory_space_constraint(array, pltpu.VMEM) for array in arrays]
 
 
-def back_kernel(dpre_ref, weight_ref, other_weight_ref, back_ref):
+def back_kernel(dpre_ref, weight_ref, other_weight_ref, back_hbm, back_ref, done):
     half = other_weight_ref.shape[1]
+    piece = half // 2
     core = lax.axis_index("tensor") % 2
-    columns = pl.ds(pl.multiple_of(core * half, half), half)
-    total = contract(dpre_ref[core], weight_ref[columns, :], 1, 1)
-    total += contract(dpre_ref[1 - core], other_weight_ref[1 - core], 1, 1)
-    back_ref[...] = total.astype(jnp.bfloat16).reshape(back_ref.shape)
+    copies = []
+    for index in range(2):
+        start = index * piece
+        columns = pl.ds(pl.multiple_of(core * half + start, piece), piece)
+        total = contract(dpre_ref[core], weight_ref[columns, :], 1, 1)
+        total += contract(dpre_ref[1 - core], other_weight_ref[1 - core, start : start + piece, :], 1, 1)
+        rows = total.astype(jnp.bfloat16).reshape(back_ref.shape[0], 2, piece)
+        back_ref[:, :, start : start + piece] = rows
+        copies.append(copy_lanes(back_ref, back_hbm, start, piece, done.at[index]))
+    for copy in copies:
+        copy.wait()
 
 
 def chip_sums(dpre, weight_in, other_weights):
@@ -138,8 +158,12 @@
     return pl.pallas_call(
         back_kernel,
         in_specs=[pl.BlockSpec(memory_space=pltpu.VMEM)] * 3,
-        out_specs=pl.BlockSpec(memory_space=pltpu.VMEM),
+        out_specs=pl.BlockSpec(memory_space=pl.ANY),
         out_shape=jax.ShapeDtypeStruct((slot_count // 2, 2, half), jnp.bfloat16),
+        scratch_shapes=[
+            pltpu.VMEM((slot_count // 2, 2, half), jnp.bfloat16),
+            pltpu.SemaphoreType.DMA((2,)),
+        ],
         name="chip_sums",
     )(*in_vmem(dpre, weight_in, other_weights))
 

time: 102 us -> 102 us (level)
  no operation moved by 1% of the time
where the time goes in v5:
time: 102 us; the launch traced here: 101 us
  blocking collectives  33.7 us (33%)
  waiting for transfers between devices  28.5 us (28%)
  starting transfers between devices  27.4 us (27%)
  Pallas kernels  5.2 us (5%)
  matrix products  3.61 us (4%)
  local copies, waits for them, and re-layouts  1.33 us (1%)
    all_to_all x2, waiting for transfers between devices, exchange(): lax.all_to_all(chunks, 'expert', split_axis=0, concat_axis=0, axis_index_...  28.5 us
    all_to_all x2, starting transfers between devices, exchange(): lax.all_to_all(chunks, 'expert', split_axis=0, concat_axis=0, axis_index_...  27.4 us
    all_to_all x1, blocking collectives, local(): lax.all_to_all(packed, 'tensor', split_axis=0, concat_axis=0, tiled=True)  16.8 us
    all_gather x1, blocking collectives, local(): joined = lax.all_gather(mine, 'tensor', axis_index_groups=teams, axis=0)  12.1 us
    dot_general x4, matrix products, contract(): lax.dot_general(left, right, (((left_dim,), (right_dim,)), ((), ())), pre...  3.18 us
    all_gather x1, blocking collectives, local(): lax.all_gather(give_weight, 'tensor', axis_index_groups=chips, axis=0)  2.95 us
    pallas_call x1, Pallas kernels, pick_rows(): pl.pallas_call(pick_kernel, in_specs=[anywhere] * 4, out_specs=[anywhere,...  2.31 us
  transfers between devices with their start and end apart: 2, of which 2 were waited for; matrix products, arithmetic and copies ran while one was open for 4% of the time, Pallas kernels for 1%

profile of v5, /device:TPU:1, one launch (start us, length us, event | category | flops | bytes accessed | tf_op | source)
XLA Modules:
  0.0 101.1 jit_solution(5239434429056358434)
XLA Ops:
  0.6 0.0 copy-start.1
  0.6 2.3 %pick_rows.1 = (bf16[64,2,768]{2,1,0:T(2,128)(2,1)}, bf16[128,64]{1,0:T(8,128)(2,1)S(1)}) custom-call(s32[64,128]{1,0:T(8,128)} %slots_hbm.1, bf16[64,1536]{1,0:T(8,128)(2,1)} %tokens_hbm.1, s32[12,64]{1,0:T(8,128)} %bitcast.51, bf16[64,1536]{1,0:T(8,128)(2,1)} %grads_hbm.1), custom_call_target="tpu_custom_call" | custom-call | tf_op jit(solution)/shard_map/pick_rows/pallas_call | solution.py:98
  3.0 22.8 %all-to-all-start = ((bf16[64,2,768]{2,1,0:T(2,128)(2,1)}), bf16[64,2,768]{2,1,0:T(2,128)(2,1)S(1)}, u32[]{:S(2)}, u32[]{:S(2)}) async-start(bf16[64,2,768]{2,1,0:T(2,128)(2,1)} %get-tuple-element.42), calls=%async_computation | async-start | bytes 393216 | tf_op jit(solution)/shard_map/all_to_all | solution.py:213
  25.8 0.0 copy-done.1
  25.8 0.1 constant_dynamic-slice_fusion
  25.9 0.1 copy.16
  26.0 0.1 broadcast_bitcast_fusion
  26.0 0.7 fusion.15
  26.7 1.2 %hold.1 = bf16[256,1536]{1,0:T(8,128)(2,1)S(1)} custom-call(bf16[256,1536]{1,0:T(8,128)(2,1)} %bitcast.50), custom_call_target="tpu_custom_call" | custom-call | tf_op jit(solution)/shard_map/hold/pallas_call | solution.py:125
  28.0 0.2 convert_reduce_fusion
  28.2 0.1 fusion.14
  28.2 0.0 copy-done.2
  28.2 0.1 select_reduce_fusion.1
  28.4 3.0 %all_gather.16.other_weight_ref = bf16[2,768,256]{2,1,0:T(8,128)(2,1)S(1)} all-gather(bf16[1,768,256]{2,1,0:T(8,128)(2,1)S(1)} %constant_dynamic-slice_fusion.1), channel_id=1, replica_groups={{0,1},{2,3},{4,5},{6,7},{8,9},{10,11},{12,13},{14,15},{16,17},{18,19},{..., dimensions={0}, use_global_device_ids=true | all-gather | bytes 1179648 | tf_op jit(solution)/shard_map/all_gather | solution.py:226
  31.3 12.1 %all-to-all-done = bf16[64,2,768]{2,1,0:T(2,128)(2,1)S(1)} async-done(((bf16[64,2,768]{2,1,0:T(2,128)(2,1)}), bf16[64,2,768]{2,1,0:T(2,128)(2,1)S(1)}, u32[]{:S(2)}, u32[]{:S(2)}) %all-to-all-start) | async-done | bytes 196640 | tf_op jit(solution)/shard_map/all_to_all | solution.py:213
  43.5 0.1 reshape.237
  43.6 12.1 %all-gather = bf16[512,768]{1,0:T(8,128)(2,1)S(1)} all-gather(bf16[128,768]{1,0:T(8,128)(2,1)S(1)} %reshape.237), channel_id=2, replica_groups={{0,1,2,3},{4,5,6,7},{8,9,10,11},{12,13,14,15},{16,17,18,19},{20,21,22,2..., dimensions={0}, use_global_device_ids=true | all-gather | bytes 983040 | tf_op jit(solution)/shard_map/all_gather | solution.py:230
  55.6 0.1 slice_bitcast_fusion.3
  55.7 0.4 fusion.9
  56.1 0.4 fusion.7
  56.5 1.9 %all-gather.1 = bf16[256,256]{1,0:T(8,128)(2,1)S(1)} all-gather(bf16[128,256]{1,0:T(8,128)(2,1)S(1)} %get-tuple-element.62), channel_id=3, replica_groups={{0,1},{2,3},{4,5},{6,7},{8,9},{10,11},{12,13},{14,15},{16,17},{18,19},{..., dimensions={0}, use_global_device_ids=true | all-gather | bytes 196608 | tf_op jit(solution)/shard_map/all_gather | solution.py:244
  58.4 1.0 %chip_sums.1 = bf16[64,2,768]{2,1,0:T(2,128)(2,1)} custom-call(bf16[2,128,256]{2,1,0:T(8,128)(2,1)S(1)} %bitcast.47, bf16[1536,256]{1,0:T(8,128)(2,1)S(1)} %bitcast.46, bf16[2,768,256]{2,1,0:T(8,128)(2,1)S(1)} %all_gather.16.other_weight_ref), custom_call_target="tpu_custom_call" | custom-call | tf_op jit(solution)/shard_map/chip_sums/pallas_call | solution.py:158
  59.5 4.6 %all-to-all-start.1 = ((bf16[64,2,768]{2,1,0:T(2,128)(2,1)}), bf16[64,2,768]{2,1,0:T(2,128)(2,1)S(1)}, u32[]{:S(2)}, u32[]{:S(2)}) async-start(bf16[64,2,768]{2,1,0:T(2,128)(2,1)} %chip_sums.1), calls=%async_computation.1 | async-start | bytes 393216 | tf_op jit(solution)/shard_map/all_to_all | solution.py:213
  64.1 0.1 select_reduce_fusion
  64.3 1.3 %convolution_convert_fusion = bf16[1536,256]{1,0:T(8,128)(2,1)} fusion(bf16[128,256]{1,0:T(8,128)(2,1)S(1)} %get-tuple-element.62, bf16[128,384]{1,0:T(8,128)(2,1)S(1)} %get-tuple-element.55, bf16[128,384]{1,0:T(8,128)(2,1)S(1)} %get-tuple-element.56, bf16[128,384]{1,0:T(8,128)(2,1)S(1)} %get-tuple-element.57, bf16[128,384]{1,0:T(8,128)(2,1)S(1)} %get-tuple-element.54), kind=kOutput, calls=%fused_computation | convolution fusion | flops 102629376 | bytes 1245184 | tf_op jit(solution)/shard_map/dot_general | solution.py:10
  65.6 1.3 %convolution_convert_fusion.1 = bf16[256,1536]{1,0:T(8,128)(2,1)} fusion(f32[128]{0:T(128)S(1)} %select_reduce_fusion.1, bf16[128,384]{1,0:T(8,128)(2,1)S(1)} %get-tuple-element.58, bf16[128,384]{1,0:T(8,128)(2,1)S(1)} %get-tuple-element.59, bf16[128,384]{1,0:T(8,128)(2,1)S(1)} %get-tuple-element.60, bf16[128,384]{1,0:T(8,128)(2,1)S(1)} %get-tuple-element.61, ...), kind=kOutput, calls=%fused_computation.1 | convolution fusion | flops 103317504 | bytes 1311232 | tf_op jit(solution)/shard_map/dot_general | solution.py:10
  66.9 16.4 %all-to-all-done.1 = bf16[64,2,768]{2,1,0:T(2,128)(2,1)S(1)} async-done(((bf16[64,2,768]{2,1,0:T(2,128)(2,1)}), bf16[64,2,768]{2,1,0:T(2,128)(2,1)S(1)}, u32[]{:S(2)}, u32[]{:S(2)}) %all-to-all-start.1) | async-done | bytes 196640 | tf_op jit(solution)/shard_map/all_to_all | solution.py:213
  83.3 0.1 reshape.238
  83.4 0.2 convolution_convert_fusion.2
  83.6 0.1 pad_maximum_fusion.2
  83.7 16.8 %all_to_all.15.arrived_ref = bf16[16,4,896]{2,1,0:T(4,128)(2,1)S(1)} all-to-all(bf16[16,4,896]{2,1,0:T(4,128)(2,1)S(1)} %pad_maximum_fusion.2), channel_id=1, replica_groups=mesh['expert'=64,'tensor'=16] {'tensor'}, dimensions={0} | all-to-all | bytes 229376 | tf_op jit(solution)/shard_map/all_to_all | solution.py:268
  100.5 0.6 finish.1
  (12 shorter events, 0.2 us)
Async XLA Ops:
  0.6 25.1 %copy-start.1 = (s32[64,12]{0,1:T(8,128)S(1)}, s32[64,12]{0,1:T(8,128)}, u32[]{:S(2)}) copy-start(s32[64,12]{0,1:T(8,128)} %param.12) | copy-start | bytes 9220
  3.0 40.5 %all-to-all-start = ((bf16[64,2,768]{2,1,0:T(2,128)(2,1)}), bf16[64,2,768]{2,1,0:T(2,128)(2,1)S(1)}, u32[]{:S(2)}, u32[]{:S(2)}) async-start(bf16[64,2,768]{2,1,0:T(2,128)(2,1)} %get-tuple-element.42), calls=%async_computation | async-start | bytes 393216 | tf_op jit(solution)/shard_map/all_to_all | solution.py:213
  26.7 1.5 %copy-start.2 = (f32[1,128]{1,0:T(1,128)S(1)}, f32[1,128]{1,0:T(1,128)}, u32[]{:S(2)}) copy-start(f32[1,128]{1,0:T(1,128)} %param.15) | copy-start | bytes 1540
  26.7 1.6 %copy-start = (bf16[1,1536,256]{2,1,0:T(8,128)(2,1)S(1)}, bf16[1,1536,256]{2,1,0:T(8,128)(2,1)}, u32[]{:S(2)}) copy-start(bf16[1,1536,256]{2,1,0:T(8,128)(2,1)} %param.16) | copy-start | bytes 2359300
  59.5 23.8 %all-to-all-start.1 = ((bf16[64,2,768]{2,1,0:T(2,128)(2,1)}), bf16[64,2,768]{2,1,0:T(2,128)(2,1)S(1)}, u32[]{:S(2)}, u32[]{:S(2)}) async-start(bf16[64,2,768]{2,1,0:T(2,128)(2,1)} %chip_sums.1), calls=%async_computation.1 | async-start | bytes 393216 | tf_op jit(solution)/shard_map/all_to_all | solution.py:213
